TPU v7x, 32 devices: a whole 2x2x4 slice. The times are simulated.
32 devices in a mesh: lon: 16 (over z, y, core), lat: 2 (over x).
Axes of the slice: x: 2, y: 2, z: 4, core: 2. Of those that a mesh axis runs over, the one named last changes fastest.
Arguments:
- fields: bfloat16 [2, 12, 192, 192], P(None, 'lat', 'lon'), may hold values from -6 to 6
- cotangent: bfloat16 [2, 12, 192, 192], P(None, 'lat', 'lon'), may hold values from -6 to 6
- land_sea: int32 [12, 192], P('lat', 'lon'), may hold values 0 or 1
- orography: int32 [12, 192], P('lat', 'lon'), may hold values from 0 to 15
- land_vec: float32 [192], replicated, may hold values from -4 to 4
- orog_table: float32 [16, 192], replicated, may hold values from -4 to 4
- gain_attn: float32 [192], replicated, may hold values from 0.1 to 1.9
- w_qkv: bfloat16 [192, 576], replicated, may hold values from -0.4375 to 0.4375
- w_proj: bfloat16 [192, 192], replicated, may hold values from -0.4375 to 0.4375
- gain_mlp: float32 [192], replicated, may hold values from 0.1 to 1.9
- w_in: bfloat16 [192, 768], replicated, may hold values from -0.4375 to 0.4375
- w_out: bfloat16 [768, 192], replicated, may hold values from -0.21875 to 0.21875
- gain_merge: float32 [768], replicated, may hold values from 0.1 to 1.9
- w_merge: bfloat16 [768, 384], replicated, may hold values from -0.21875 to 0.21875
- gain_coarse: float32 [384], replicated, may hold values from 0.1 to 1.9
- w_cqkv: bfloat16 [384, 1152], replicated, may hold values from -0.3125 to 0.3125
- w_cproj: bfloat16 [384, 384], replicated, may hold values from -0.3125 to 0.3125
- w_up: bfloat16 [384, 768], replicated, may hold values from -0.3125 to 0.3125
Outputs:
- prediction: bfloat16 [2, 12, 192, 192], P(None, 'lat', 'lon')
- grad_input: bfloat16 [2, 12, 192, 192], P(None, 'lat', 'lon')
- grad_qkv: float32 [192, 576], replicated
- grad_proj: float32 [192, 192], replicated
All inputs are finite; a program needn't handle non-finite values. No bound on the sum of `land_sea` on one device may be relied on, other than what follows from the above.
Results may differ from a plain program's by a relative error of at most 0.013.
Values may be sent and summed in bfloat16 or wider, within the bound.
A program may use at most 64 MiB of HBM per device.

v0:
```python
import math

import jax
import jax.numpy as jnp
from jax import lax
from jax.sharding import PartitionSpec as P

HEADS_F = 6
HEADS_C = 12
WLAT = 6
WLON = 12


epsilon = 1e-05
gelu_coeff = 0.7978845608028654


def from_behind(block, axis, distance):
    devices = range(lax.axis_size(axis))
    route = [((i - distance) % len(devices), i) for i in devices]
    return lax.ppermute(block, axis, route)


def swapped(x, axis, stride):
    return lax.ppermute(x, axis, [(i, i ^ 1 << stride) for i in range(lax.axis_size(axis))])


def shortened(x):

    def short(part):
        return part.astype(jnp.bfloat16) if part.dtype == jnp.float32 else part

    return jax.tree.map(short, x)


def layer_norm(values, gain_vec):
    average = jnp.mean(values, axis=-1, keepdims=True)
    centred = values - average
    spread = jnp.mean(centred * centred, axis=-1, keepdims=True)
    return centred * lax.rsqrt(spread + epsilon) * gain_vec


def layer_norm_back(values, gain_vec, upstream):
    average = jnp.mean(values, axis=-1, keepdims=True)
    centred = values - average
    spread = jnp.mean(centred * centred, axis=-1, keepdims=True)
    inverse = lax.rsqrt(spread + epsilon)
    normal = centred * inverse
    scaled = upstream * gain_vec
    return inverse * (
        scaled
        - jnp.mean(scaled, axis=-1, keepdims=True)
        - normal * jnp.mean(scaled * normal, axis=-1, keepdims=True)
    )


def gelu_tanh(values):
    inner = gelu_coeff * (values + 0.044715 * values * values * values)
    return 0.5 * values * (1.0 + jnp.tanh(inner))


def gelu_slope(values):
    inner = gelu_coeff * (values + 0.044715 * values * values * values)
    tangent = jnp.tanh(inner)
    return 0.5 * (1.0 + tangent) + 0.5 * values * (1.0 - tangent * tangent) * gelu_coeff * (
        1.0 + 3.0 * 0.044715 * values * values
    )


def embed(fields, land_sea, orography, land_vec, orog_table):
    classes = (orography[..., None] == jnp.arange(orog_table.shape[0], dtype=jnp.int32)).astype(
        jnp.float32
    )
    lookup = jnp.dot(classes, orog_table, precision=lax.Precision.HIGHEST)
    surface = land_sea.astype(jnp.float32)[..., None] * land_vec + lookup
    return fields.astype(jnp.float32) + surface[None]


def merge_cells(tensor):
    levels, lat_rows, lon_cols, feature = tensor.shape
    tensor = tensor.reshape(levels, lat_rows // 2, 2, lon_cols // 2, 2, feature).transpose(
        0, 1, 3, 2, 4, 5
    )
    return tensor.reshape(levels, lat_rows // 2, lon_cols // 2, 4 * feature)


def split_cells(tensor):
    levels, lat_rows, lon_cols, wide = tensor.shape
    tensor = tensor.reshape(levels, lat_rows, lon_cols, 2, 2, wide // 4).transpose(0, 1, 3, 2, 4, 5)
    return tensor.reshape(levels, lat_rows * 2, lon_cols * 2, wide // 4)


def to_windows(tensor, win_rows, win_cols):
    levels, lat_rows, lon_cols, feature = tensor.shape
    tensor = tensor.reshape(
        levels // 2, 2, lat_rows // win_rows, win_rows, lon_cols // win_cols, win_cols, feature
    )
    tensor = tensor.transpose(0, 2, 4, 1, 3, 5, 6)
    return tensor.reshape(-1, 2 * win_rows * win_cols, feature)


def from_windows(tensor, levels, lat_rows, lon_cols, win_rows, win_cols):
    feature = tensor.shape[-1]
    tensor = tensor.reshape(
        levels // 2, lat_rows // win_rows, lon_cols // win_cols, 2, win_rows, win_cols, feature
    )
    return tensor.transpose(0, 3, 1, 4, 2, 5, 6).reshape(levels, lat_rows, lon_cols, feature)


def fine_mask(first_band):
    row_ids = jnp.arange(2 * WLAT * WLON, dtype=jnp.int32) // WLON % WLAT
    region = jnp.logical_and(first_band, row_ids < WLAT // 2)
    return (region[:, None] == region[None, :])[None, None]


def split_heads(tensor, heads):
    return tensor.reshape(tensor.shape[0], tensor.shape[1], heads, -1)


def attend_probs(queries, keys_in, allowed, heads):
    query_heads = split_heads(queries, heads)
    key_heads = split_heads(keys_in, heads)
    scores = jnp.einsum(
        "wqhd,wkhd->whqk", query_heads, key_heads, preferred_element_type=jnp.float32
    ) / math.sqrt(query_heads.shape[-1])
    if allowed is not None:
        scores = jnp.where(allowed, scores, -1e30)
    top = jnp.max(scores, axis=-1, keepdims=True)
    expon = jnp.exp(scores - top)
    return expon / jnp.sum(expon, axis=-1, keepdims=True)


def attend(queries, keys_in, values, allowed, heads):
    soft_bf = attend_probs(queries, keys_in, allowed, heads).astype(jnp.bfloat16)
    value_heads = split_heads(values, heads)
    mixed = jnp.einsum("whqk,wkhd->wqhd", soft_bf, value_heads, preferred_element_type=jnp.float32)
    return mixed.reshape(queries.shape[0], queries.shape[1], -1).astype(jnp.bfloat16)


def attend_back(queries, keys_in, values, allowed, heads, grad_out):
    probs = attend_probs(queries, keys_in, allowed, heads)
    soft_bf = probs.astype(jnp.bfloat16)
    query_heads = split_heads(queries, heads)
    key_heads = split_heads(keys_in, heads)
    value_heads = split_heads(values, heads)
    grad_heads = split_heads(grad_out, heads)
    root = math.sqrt(query_heads.shape[-1])
    grad_values = jnp.einsum(
        "whqk,wqhd->wkhd", soft_bf, grad_heads, preferred_element_type=jnp.float32
    )
    grad_soft = jnp.einsum(
        "wqhd,wkhd->whqk", grad_heads, value_heads, preferred_element_type=jnp.float32
    )
    grad_scores = probs * (grad_soft - jnp.sum(grad_soft * probs, axis=-1, keepdims=True))
    score_bf = grad_scores.astype(jnp.bfloat16)
    grad_queries = (
        jnp.einsum("whqk,wkhd->wqhd", score_bf, key_heads, preferred_element_type=jnp.float32)
        / root
    )
    grad_keys = (
        jnp.einsum("whqk,wqhd->wkhd", score_bf, query_heads, preferred_element_type=jnp.float32)
        / root
    )
    windows = queries.shape[0]
    return (
        grad_queries.reshape(windows, queries.shape[1], -1),
        grad_keys.reshape(windows, keys_in.shape[1], -1),
        grad_values.reshape(windows, keys_in.shape[1], -1),
    )


def roll_in(tensor):
    half_cols = tensor.shape[2] // 2
    half_rows = tensor.shape[1] // 2
    arriving = from_behind(tensor[:, :, half_cols:], "lon", 1)
    shifted = jnp.concatenate([arriving, tensor[:, :, :half_cols]], axis=2)
    incoming = from_behind(shifted[:, half_rows:], "lat", 1)
    return jnp.concatenate([incoming, shifted[:, :half_rows]], axis=1)


def roll_out(tensor):
    half_cols = tensor.shape[2] // 2
    half_rows = tensor.shape[1] // 2
    incoming = from_behind(tensor[:, :half_rows], "lat", -1)
    shifted = jnp.concatenate([tensor[:, half_rows:], incoming], axis=1)
    arriving = from_behind(shifted[:, :, :half_cols], "lon", -1)
    return jnp.concatenate([shifted[:, :, half_cols:], arriving], axis=2)


def per_device(
    fields,
    cotangent,
    land_sea,
    orography,
    land_vec,
    orog_table,
    gain_attn,
    w_qkv,
    w_proj,
    gain_mlp,
    w_in,
    w_out,
    gain_merge,
    w_merge,
    gain_coarse,
    w_cqkv,
    w_cproj,
    w_up,
):
    levels, lat_rows, lon_cols, channels = fields.shape
    coarse = w_cproj.shape[0]
    base_field = embed(fields, land_sea, orography, land_vec, orog_table)
    normed = layer_norm(base_field, gain_attn).astype(jnp.bfloat16)
    rolled = roll_in(normed)
    allowed = fine_mask(lax.axis_index("lat") == 0)
    fine_qkv = jnp.dot(rolled, w_qkv, preferred_element_type=jnp.float32).astype(jnp.bfloat16)
    windows = to_windows(fine_qkv, WLAT, WLON)
    queries = windows[..., :channels]
    keys_in = windows[..., channels : 2 * channels]
    values = windows[..., 2 * channels :]
    attended = attend(queries, keys_in, values, allowed, HEADS_F)
    restored = roll_out(from_windows(attended, levels, lat_rows, lon_cols, WLAT, WLON))
    first_res = base_field + jnp.dot(restored, w_proj, preferred_element_type=jnp.float32)
    mlp_in = layer_norm(first_res, gain_mlp).astype(jnp.bfloat16)
    pre_act = jnp.dot(mlp_in, w_in, preferred_element_type=jnp.float32)
    active = gelu_tanh(pre_act).astype(jnp.bfloat16)
    second_res = first_res + jnp.dot(active, w_out, preferred_element_type=jnp.float32)
    merged = merge_cells(second_res)
    merge_in = layer_norm(merged, gain_merge).astype(jnp.bfloat16)
    coarse_base = jnp.dot(merge_in, w_merge, preferred_element_type=jnp.float32)
    coarse_norm = layer_norm(coarse_base, gain_coarse).astype(jnp.bfloat16)
    coarse_flat = coarse_norm.reshape(levels // 2, -1, coarse)
    coarse_qkv = jnp.dot(coarse_flat, w_cqkv, preferred_element_type=jnp.float32).astype(
        jnp.bfloat16
    )
    coarse_query = coarse_qkv[..., :coarse]
    own_pairs = coarse_qkv[..., coarse:]
    pair_kv = jnp.concatenate([own_pairs, swapped(own_pairs, "lat", 0)], axis=1)
    group_kv = jnp.concatenate([pair_kv, swapped(pair_kv, "lon", 0)], axis=1)
    group_keys = group_kv[..., :coarse]
    group_values = group_kv[..., coarse:]
    coarse_out = attend(coarse_query, group_keys, group_values, None, HEADS_C).reshape(
        coarse_base.shape
    )
    coarse_next = coarse_base + jnp.dot(coarse_out, w_cproj, preferred_element_type=jnp.float32)
    upward = jnp.dot(coarse_next.astype(jnp.bfloat16), w_up, preferred_element_type=jnp.float32)
    final = second_res + split_cells(upward)
    prediction = final.astype(jnp.bfloat16)
    grad_up = merge_cells(cotangent)
    grad_cnext = jnp.dot(grad_up, w_up.T, preferred_element_type=jnp.float32)
    grad_cout = jnp.dot(
        grad_cnext.astype(jnp.bfloat16), w_cproj.T, preferred_element_type=jnp.float32
    ).astype(jnp.bfloat16)
    cout_flat = grad_cout.reshape(levels // 2, -1, coarse)
    grad_cq, grad_gk, grad_gv = attend_back(
        coarse_query, group_keys, group_values, None, HEADS_C, cout_flat
    )
    grad_group = jnp.concatenate([grad_gk, grad_gv], axis=-1)
    half_keys = grad_group.shape[1] // 2
    returned = swapped(grad_group[:, half_keys:].astype(jnp.bfloat16), "lon", 0).astype(jnp.float32)
    grad_pair = grad_group[:, :half_keys] + returned
    own_keys = half_keys // 2
    grad_kv = grad_pair[:, :own_keys] + swapped(shortened(grad_pair[:, own_keys:]), "lat", 0)
    grad_cqkv = jnp.concatenate([grad_cq, grad_kv], axis=-1).astype(jnp.bfloat16)
    grad_cnorm = jnp.dot(grad_cqkv, w_cqkv.T, preferred_element_type=jnp.float32).reshape(
        coarse_base.shape
    )
    grad_cbase = grad_cnext + layer_norm_back(coarse_base, gain_coarse, grad_cnorm)
    grad_merge_in = jnp.dot(
        grad_cbase.astype(jnp.bfloat16), w_merge.T, preferred_element_type=jnp.float32
    )
    grad_second = cotangent.astype(jnp.float32) + split_cells(
        layer_norm_back(merged, gain_merge, grad_merge_in)
    )
    grad_active = jnp.dot(
        grad_second.astype(jnp.bfloat16), w_out.T, preferred_element_type=jnp.float32
    )
    grad_pre = (grad_active * gelu_slope(pre_act)).astype(jnp.bfloat16)
    grad_mlp_in = jnp.dot(grad_pre, w_in.T, preferred_element_type=jnp.float32)
    grad_first = grad_second + layer_norm_back(first_res, gain_mlp, grad_mlp_in)
    grad_first_bf = grad_first.astype(jnp.bfloat16)
    proj_local = jnp.dot(
        restored.reshape(-1, channels).T,
        grad_first_bf.reshape(-1, channels),
        preferred_element_type=jnp.float32,
    )
    grad_restored = jnp.dot(grad_first_bf, w_proj.T, preferred_element_type=jnp.float32).astype(
        jnp.bfloat16
    )
    grad_attended = roll_in(grad_restored)
    grad_q, grad_k, grad_v = attend_back(
        queries, keys_in, values, allowed, HEADS_F, to_windows(grad_attended, WLAT, WLON)
    )
    joined = jnp.concatenate([grad_q, grad_k, grad_v], axis=-1).astype(jnp.bfloat16)
    grad_fqkv = from_windows(joined, levels, lat_rows, lon_cols, WLAT, WLON)
    qkv_local = jnp.dot(
        rolled.reshape(-1, channels).T,
        grad_fqkv.reshape(-1, 3 * channels),
        preferred_element_type=jnp.float32,
    )
    grad_rolled = jnp.dot(grad_fqkv, w_qkv.T, preferred_element_type=jnp.float32).astype(
        jnp.bfloat16
    )
    grad_normed = roll_out(grad_rolled)
    grad_base = grad_first + layer_norm_back(base_field, gain_attn, grad_normed.astype(jnp.float32))
    grad_qkv, grad_proj = lax.psum((qkv_local, proj_local), ("lon", "lat"))
    return (prediction, grad_base.astype(jnp.bfloat16), grad_qkv, grad_proj)


def solution(mesh):
    placed = (
        P(None, "lat", "lon", None),
        P(None, "lat", "lon", None),
        P("lat", "lon"),
        P("lat", "lon"),
        P(),
        P(),
        P(),
        P(),
        P(),
        P(),
        P(),
        P(),
        P(),
        P(),
        P(),
        P(),
        P(),
        P(),
    )
    return jax.shard_map(
        per_device,
        mesh=mesh,
        in_specs=placed,
        out_specs=(P(None, "lat", "lon", None), P(None, "lat", "lon", None), P(), P()),
        check_vma=False,
    )
```

profile of v0, /device:TPU:0, one launch (start us, length us, event | category | flops | bytes accessed | tf_op | source)
XLA Modules:
  0.0 226.9 jit_solution(13723473107947890946)
XLA Ops:
  7.3 0.8 convert_element_type.137
  8.0 0.9 convolution_add_fusion.2
  9.3 0.7 copy-done.56
  11.1 6.7 %collective-permute-done = bf16[2,6,6,192]{3,2,1,0:T(8,128)(2,1)S(1)} collective-permute-done((bf16[2,6,6,192]{3,2,1,0:T(8,128)(2,1)S(1)}, bf16[2,6,6,192]{3,2,1,0:T(8,128)(2,1)S(1)}, u32[]{:S(2)}, u32[]{:S(2)}) %collective-permute-start) | collective-permute-done | bytes 27680 | tf_op jit(solution)/shard_map/ppermute | solution.py:21
  17.9 2.0 collective-permute-start.1
  20.0 2.1 collective-permute-done.1
  22.9 1.4 fusion.144
  25.4 2.0 collective-permute-start.2
  27.4 2.2 collective-permute-done.2
  29.6 0.8 copy-done.25
  30.6 0.8 collective-permute-done.3
  33.5 0.8 copy-done.16
  39.1 2.0 collective-permute-start.4
  41.4 2.0 collective-permute-done.4
  43.4 0.7 pad_maximum_fusion.2
  44.4 0.8 copy.164
  45.3 0.7 reshape.451
  46.3 0.8 copy.154
  47.6 2.3 %fusion.83 = f32[12,32,144]{2,1,0:T(8,128)} fusion(bf16[36,12,32]{0,2,1:T(8,128)(2,1)} %copy.164, f32[12,36]{1,0:T(8,128)S(1)} %get-tuple-element.53, bf16[36,12,32]{0,2,1:T(8,128)(2,1)S(1)} %bitcast.179, bf16[144,12,32]{0,2,1:T(8,128)(2,1)S(1)} %bitcast.174), kind=kOutput, calls=%fused_computation.134 | convolution fusion | flops 8212031 | bytes 388800 | tf_op jit(solution)/shard_map/whqk,wqhd->wkhd/dot_general | solution.py:148
  50.0 1.1 copy.169
  51.1 1.3 multiply_reduce_fusion.1
  52.5 1.2 multiply_convert_fusion.2
  53.7 0.9 convolution_multiply_fusion.3
  54.7 1.1 copy.168
  56.8 0.8 fusion.16
  57.7 2.0 collective-permute-start.7
  59.7 1.5 fusion.15
  61.5 0.7 copy-done.24
  62.8 0.6 copy-done.37
  67.0 1.6 fusion.135
  68.9 0.7 copy-done.19
  71.3 5.0 %collective-permute-done.8 = bf16[2,6,6,192]{3,2,1,0:T(8,128)(2,1)S(1)} collective-permute-done((bf16[2,6,6,192]{3,2,1,0:T(8,128)(2,1)S(1)}, bf16[2,6,6,192]{3,2,1,0:T(8,128)(2,1)S(1)}, u32[]{:S(2)}, u32[]{:S(2)}) %collective-permute-start.8) | collective-permute-done | bytes 27680 | tf_op jit(solution)/shard_map/ppermute | solution.py:21
  76.3 1.5 collective-permute-start.9
  77.8 0.7 copy.189
  78.5 2.0 collective-permute-done.9
  80.9 0.7 copy-done.21
  81.6 1.5 convolution_convert_fusion.3
  85.3 0.8 copy-done.30
  86.4 1.5 collective-permute-start.10
  87.9 0.9 convolution_bitcast_fusion
  88.8 1.8 collective-permute-done.10
  90.7 0.8 copy-done.42
  91.4 1.1 fusion.40
  92.6 0.6 copy-done.35
  93.7 0.7 copy.190
  94.4 123.1 %all-reduce.3.cloned.1.call-done = (f32[192,576]{1,0:T(8,128)}, f32[192,192]{1,0:T(8,128)}) async-done(((f32[192,576]{1,0:T(8,128)}, f32[192,192]{1,0:T(8,128)}), (f32[192,576]{1,0:T(8,128)}, f32[192,192]{1,0:T(8,128)})) %all-reduce.3.cloned.1.call-update) | async-done | bytes 589840 | tf_op jit(solution)/shard_map/psum | solution.py:306
  217.5 1.9 copy.237
  219.3 0.7 copy.238
  (252 shorter events, 22.6 us)
Async XLA Ops:
  7.2 31.6 %copy-start = (bf16[384,1152]{1,0:T(8,128)(2,1)S(1)}, bf16[384,1152]{1,0:T(8,128)(2,1)}, u32[]{:S(2)}) copy-start(bf16[384,1152]{1,0:T(8,128)(2,1)} %param.33) | copy-start | bytes 2654212
  7.2 1.8 copy-start.1
  7.2 210.2 %all-reduce.3.cloned.1.call-start = ((), (), s32[]{:S(2)}) async-start(), calls=%async_computation | async-start | bytes 1376256 | tf_op jit(solution)/shard_map/psum | solution.py:306
  10.6 11.5 %copy-start.29 = (bf16[192,576]{1,0:T(8,128)(2,1)S(1)}, bf16[192,576]{1,0:T(8,128)(2,1)}, u32[]{:S(2)}) copy-start(bf16[192,576]{1,0:T(8,128)(2,1)} %param.25) | copy-start | bytes 663556
  10.6 7.3 %collective-permute-start = (bf16[2,6,6,192]{3,2,1,0:T(8,128)(2,1)S(1)}, bf16[2,6,6,192]{3,2,1,0:T(8,128)(2,1)S(1)}, u32[]{:S(2)}, u32[]{:S(2)}) collective-permute-start(bf16[2,6,6,192]{3,2,1,0:T(8,128)(2,1)S(1)} %get-tuple-element.45), channel_id=1, source_target_pairs={{30,0},{0,2},{2,4},{4,6},{6,8},{8,10},{10,12},{12,14},{14,16},{16,... | collective-permute-start | bytes 82952 | tf_op jit(solution)/shard_map/ppermute | solution.py:21
  17.9 4.2 %collective-permute-start.1 = (bf16[2,3,12,192]{3,2,1,0:T(8,128)(2,1)S(1)}, bf16[2,3,12,192]{3,2,1,0:T(8,128)(2,1)S(1)}, u32[]{:S(2)}, u32[]{:S(2)}) collective-permute-start(bf16[2,3,12,192]{3,2,1,0:T(8,128)(2,1)S(1)} %fusion.105), channel_id=1, source_target_pairs={{1,0},{0,1},{3,2},{2,3},{5,4},{4,5},{7,6},{6,7},{9,8},{8,9},{11,10... | collective-permute-start | bytes 82952 | tf_op jit(solution)/shard_map/ppermute | solution.py:21
  20.0 4.3 %copy-start.51 = (pred[144,144]{0,1:T(8,128)(4,1)}, pred[144,144]{0,1:T(8,128)(4,1)S(1)}, u32[]{:S(2)}) copy-start(pred[144,144]{0,1:T(8,128)(4,1)S(1)} %broadcast_compare_fusion) | copy-start | bytes 62212
  22.6 1.7 copy-start.20
  22.8 1.5 copy-start.22
  22.9 1.4 copy-start.38
  25.4 4.2 %collective-permute-start.2 = (bf16[2,3,12,192]{3,2,1,0:T(8,128)(2,1)S(1)}, bf16[2,3,12,192]{3,2,1,0:T(8,128)(2,1)S(1)}, u32[]{:S(2)}, u32[]{:S(2)}) collective-permute-start(bf16[2,3,12,192]{3,2,1,0:T(8,128)(2,1)S(1)} %get-tuple-element.44), channel_id=1, source_target_pairs={{1,0},{0,1},{3,2},{2,3},{5,4},{4,5},{7,6},{6,7},{9,8},{8,9},{11,10... | collective-permute-start | bytes 82952 | tf_op jit(solution)/shard_map/ppermute | solution.py:21
  29.6 1.8 copy-start.32
  29.6 1.8 collective-permute-start.3
  31.4 1.0 copy-start.27
  32.9 1.5 copy-start.64
  34.7 1.4 copy-start.2
  38.8 2.3 %copy-start.3 = (bf16[384,768]{1,0:T(8,128)(2,1)S(1)}, bf16[384,768]{1,0:T(8,128)(2,1)}, u32[]{:S(2)}) copy-start(bf16[384,768]{1,0:T(8,128)(2,1)} %param.35) | copy-start | bytes 1769476
  39.1 4.3 %collective-permute-start.4 = (bf16[1,36,768]{2,1,0:T(8,128)(2,1)S(1)}, bf16[1,36,768]{2,1,0:T(8,128)(2,1)S(1)}, u32[]{:S(2)}, u32[]{:S(2)}) collective-permute-start(bf16[1,36,768]{2,1,0:T(8,128)(2,1)S(1)} %slice.121), channel_id=1, source_target_pairs={{0,1},{1,0},{2,3},{3,2},{4,5},{5,4},{6,7},{7,6},{8,9},{9,8},{10,11... | collective-permute-start | bytes 165896 | tf_op jit(solution)/shard_map/ppermute | solution.py:25
  41.1 3.0 %copy-start.7 = (bf16[384,384]{1,0:T(8,128)(2,1)S(1)}, bf16[384,384]{1,0:T(8,128)(2,1)}, u32[]{:S(2)}) copy-start(bf16[384,384]{1,0:T(8,128)(2,1)} %param.34) | copy-start | bytes 884740
  41.4 2.7 %copy-start.14 = (f32[2,3,6,384]{3,2,1,0:T(8,128)}, f32[2,3,6,384]{3,2,1,0:T(8,128)S(1)}, u32[]{:S(2)}) copy-start(f32[2,3,6,384]{3,2,1,0:T(8,128)S(1)} %fusion.29) | copy-start | bytes 165892
  44.1 2.0 collective-permute-start.5
  46.1 7.6 %copy-start.10 = (bf16[1,36,384]{1,2,0:T(8,128)(2,1)}, bf16[1,36,384]{1,2,0:T(8,128)(2,1)S(1)}, u32[]{:S(2)}) copy-start(bf16[1,36,384]{1,2,0:T(8,128)(2,1)S(1)} %copy.206) | copy-start | bytes 82948
  46.3 1.3 copy-start.5
  47.6 3.5 %copy-start.4 = (f32[12,36,144]{2,1,0:T(8,128)}, f32[12,36,144]{2,1,0:T(8,128)S(1)}, u32[]{:S(2)}) copy-start(f32[12,36,144]{2,1,0:T(8,128)S(1)} %get-tuple-element.54) | copy-start | bytes 746500
  47.6 4.9 %copy-start.52 = (f32[12,36]{1,0:T(8,128)}, f32[12,36]{1,0:T(8,128)S(1)}, u32[]{:S(2)}) copy-start(f32[12,36]{1,0:T(8,128)S(1)} %get-tuple-element.53) | copy-start | bytes 5188
  55.9 1.7 collective-permute-start.6
  57.6 2.0 copy-start.11
  57.6 2.0 copy-start.53
  57.7 5.0 %collective-permute-start.7 = (bf16[1,36,768]{2,1,0:T(8,128)(2,1)S(1)}, bf16[1,36,768]{2,1,0:T(8,128)(2,1)S(1)}, u32[]{:S(2)}, u32[]{:S(2)}) collective-permute-start(bf16[1,36,768]{2,1,0:T(8,128)(2,1)S(1)} %slice.173), channel_id=1, source_target_pairs={{0,1},{1,0},{2,3},{3,2},{4,5},{5,4},{6,7},{7,6},{8,9},{9,8},{10,11... | collective-permute-start | bytes 165896 | tf_op jit(solution)/shard_map/ppermute | solution.py:25
  63.4 1.0 copy-start.44
  63.4 1.0 copy-start.46
  63.4 1.0 copy-start.55
  65.7 1.1 copy-start.17
  65.9 1.0 copy-start.28
  66.1 1.0 copy-start.26
  66.1 0.9 copy-start.41
  69.6 1.0 copy-start.8
  69.8 6.4 %collective-permute-start.8 = (bf16[2,6,6,192]{3,2,1,0:T(8,128)(2,1)S(1)}, bf16[2,6,6,192]{3,2,1,0:T(8,128)(2,1)S(1)}, u32[]{:S(2)}, u32[]{:S(2)}) collective-permute-start(bf16[2,6,6,192]{3,2,1,0:T(8,128)(2,1)S(1)} %get-tuple-element.39), channel_id=1, source_target_pairs={{30,0},{0,2},{2,4},{4,6},{6,8},{8,10},{10,12},{12,14},{14,16},{16,... | collective-permute-start | bytes 82952 | tf_op jit(solution)/shard_map/ppermute | solution.py:21
  71.2 6.5 %copy-start.13 = (f32[2,6,12,192]{3,2,1,0:T(8,128)S(1)}, f32[2,6,12,192]{3,2,1,0:T(8,128)}, u32[]{:S(2)}) copy-start(f32[2,6,12,192]{3,2,1,0:T(8,128)} %copy-done.12) | copy-start | bytes 331780
  76.3 4.2 %collective-permute-start.9 = (bf16[2,3,12,192]{3,2,1,0:T(8,128)(2,1)S(1)}, bf16[2,3,12,192]{3,2,1,0:T(8,128)(2,1)S(1)}, u32[]{:S(2)}, u32[]{:S(2)}) collective-permute-start(bf16[2,3,12,192]{3,2,1,0:T(8,128)(2,1)S(1)} %fusion.103), channel_id=1, source_target_pairs={{1,0},{0,1},{3,2},{2,3},{5,4},{4,5},{7,6},{6,7},{9,8},{8,9},{11,10... | collective-permute-start | bytes 82952 | tf_op jit(solution)/shard_map/ppermute | solution.py:21
  81.6 1.5 copy-start.9
  81.6 1.5 copy-start.39
  85.1 0.9 copy-start.30
  86.4 1.5 copy-start.33
  86.4 1.5 copy-start.50
  86.4 4.2 %collective-permute-start.10 = (bf16[2,3,12,192]{3,2,1,0:T(8,128)(2,1)S(1)}, bf16[2,3,12,192]{3,2,1,0:T(8,128)(2,1)S(1)}, u32[]{:S(2)}, u32[]{:S(2)}) collective-permute-start(bf16[2,3,12,192]{3,2,1,0:T(8,128)(2,1)S(1)} %get-tuple-element.38), channel_id=1, source_target_pairs={{1,0},{0,1},{3,2},{2,3},{5,4},{4,5},{7,6},{6,7},{9,8},{8,9},{11,10... | collective-permute-start | bytes 82952 | tf_op jit(solution)/shard_map/ppermute | solution.py:21
  90.6 2.0 collective-permute-start.11
  217.5 1.9 copy-start.31
  (32 other events, 24.3 us)
Sparse Core Ops, SparseCore 0:
  92.7 124.7 all-reduce.2
where the time goes:
time: 228 us; the launch traced here: 227 us
  waiting for transfers between devices  146 us (64%)
  local copies, waits for them, and re-layouts  28.2 us (12%)
  matrix products  20.2 us (9%)
  between operations  15.1 us (7%)
  starting transfers between devices  12.6 us (6%)
  other arithmetic  5.21 us (2%)
    psum x1, waiting for transfers between devices, per_device(): grad_qkv, grad_proj = lax.psum((qkv_local, proj_local), ('lon', 'lat'))  123 us
    ppermute x8, waiting for transfers between devices, from_behind(): return lax.ppermute(block, axis, route)  20.4 us
    unnamed x138, local copies, waits for them, and re-layouts  17.1 us
    ppermute x8, starting transfers between devices, from_behind(): return lax.ppermute(block, axis, route)  7.98 us
    ppermute x4, starting transfers between devices, swapped(): lax.ppermute(x, axis, [(i, i ^ 1 << stride) for i in range(lax.axis_size(...  4.57 us
  transfers between devices with their start and end apart: 13, of which 9 were waited for; matrix products, arithmetic and copies ran while one was open for 4% of the time, Pallas kernels for 0%

commit v1 on v0

v1 whole, which is shorter than its diff:
```python
import functools
import math

import jax
import jax.numpy as jnp
import numpy as np
from jax import lax
from jax.experimental import pallas as pl
from jax.experimental.pallas import tpu as pltpu
from jax.sharding import PartitionSpec as P

HEADS_F = 6
WLAT = 6
WLON = 12
PAD = 48
FINE = 4 * PAD
MESH = pl.DeviceIdType.MESH
F32 = jnp.float32
BF16 = jnp.bfloat16

epsilon = 1e-05
gelu_coeff = 0.7978845608028654


def layer_norm(values, gain_vec):
    average = jnp.mean(values, axis=-1, keepdims=True)
    centred = values - average
    spread = jnp.mean(centred * centred, axis=-1, keepdims=True)
    return centred * lax.rsqrt(spread + epsilon) * gain_vec


def layer_norm_back(values, gain_vec, upstream):
    average = jnp.mean(values, axis=-1, keepdims=True)
    centred = values - average
    spread = jnp.mean(centred * centred, axis=-1, keepdims=True)
    inverse = lax.rsqrt(spread + epsilon)
    normal = centred * inverse
    scaled = upstream * gain_vec
    return inverse * (
        scaled
        - jnp.mean(scaled, axis=-1, keepdims=True)
        - normal * jnp.mean(scaled * normal, axis=-1, keepdims=True)
    )


def gelu_tanh(values):
    inner = gelu_coeff * (values + 0.044715 * values * values * values)
    return 0.5 * values * (1.0 + jnp.tanh(inner))


def gelu_slope(values):
    inner = gelu_coeff * (values + 0.044715 * values * values * values)
    tangent = jnp.tanh(inner)
    return 0.5 * (1.0 + tangent) + 0.5 * values * (1.0 - tangent * tangent) * gelu_coeff * (
        1.0 + 3.0 * 0.044715 * values * values
    )


def orderings():
    to_parity = np.zeros((FINE, 2 * WLAT * WLON), np.float32)
    to_quadrant = np.zeros((FINE, FINE), np.float32)
    for level in range(2):
        for row in range(WLAT):
            for col in range(WLON):
                natural = (level * WLAT + row) * WLON + col
                parity = (row % 2 * 2 + col % 2) * PAD + (level * 3 + row // 2) * 6 + col // 2
                quadrant = (row // 3 * 2 + col // 6) * PAD + (level * 3 + row % 3) * 6 + col % 6
                to_parity[parity, natural] = 1
                to_quadrant[quadrant, parity] = 1
    eye = np.eye(FINE, dtype=np.float32)
    fold = np.zeros((PAD, FINE), np.float32)
    for group in range(4):
        fold[:, group * PAD : (group + 1) * PAD] = np.eye(PAD)
    return [
        jnp.asarray(m, BF16)
        for m in (to_parity, to_parity.T, to_quadrant, to_quadrant.T, eye, fold)
    ]

def dot(a, b):
    return jnp.dot(a, b, preferred_element_type=F32)

def dot_nt(a, b):
    return lax.dot_general(a, b, (((1,), (1,)), ((), ())), preferred_element_type=F32)

def iota(shape, axis):
    return lax.broadcasted_iota(jnp.int32, shape, axis)

def blocks(tensor):
    return [tensor[g * PAD : (g + 1) * PAD] for g in range(4)]

def wide_mean(parts):
    total = parts[0]
    for part in parts[1:]:
        total = total + part
    return jnp.sum(total, axis=-1, keepdims=True) * (1.0 / (4 * total.shape[-1]))

def flip(index, bit):
    return index + bit * (1 - 2 * (index // bit % 2))

def kernel(
    sizes,
    fields,
    cotangent,
    surface_in,
    table,
    gain_attn,
    w_qkv,
    w_proj,
    gain_mlp,
    w_in,
    w_out,
    gain_merge,
    w_merge,
    gain_coarse,
    w_cqkv,
    w_cproj,
    w_up,
    to_parity,
    to_natural,
    to_quadrant,
    from_quadrant,
    eye,
    fold,
    pred_out,
    gin_out,
    gqkv_out,
    gproj_out,
    norm_send,
    norm_win,
    att_win,
    att_back,
    kv,
    gkv_send,
    gkv_recv,
    gres_send,
    gres_win,
    groll_win,
    groll_back,
    probs_f,
    probs_c,
    reduce_send,
    reduce_recv,
    line_send,
    line_recv,
    gathered,
    send_sem,
    recv_sem,
):
    lat_size, lon_size, reduces = sizes
    i = lax.axis_index("lat")
    j = lax.axis_index("lon")

    def at(lat, lon):
        return (lax.rem(lon + lon_size, lon_size), lax.rem(lat + lat_size, lat_size))

    ahead = [at(i, j + 1), at(i + 1, j), at(i + 1, j + 1)]
    behind = [at(i, j - 1), at(i - 1, j), at(i - 1, j - 1)]
    group = [(flip(j, 1), i), (j, flip(i, 1)), (flip(j, 1), flip(i, 1))]
    greeted = ahead + behind + group
    plane, line = [], []
    if reduces:
        for d in range(1, 8):
            lat = flip(i, 1) if d & 4 else i
            lon = flip(j, 2) if d & 2 else j
            lon = flip(lon, 1) if d & 1 else lon
            plane.append((lon, lat))
        for d in range(1, 4):
            lon = flip(j, 8) if d & 2 else j
            lon = flip(lon, 4) if d & 1 else lon
            line.append((lon, i))
        greeted = greeted + plane + line
    barrier = pltpu.get_barrier_semaphore()
    for device in greeted:
        pl.semaphore_signal(barrier, inc=1, device_id=device, device_id_type=MESH)

    started = []

    def send(source, target, device):
        n = len(started)
        copy = pltpu.make_async_remote_copy(
            src_ref=source,
            dst_ref=target,
            send_sem=send_sem.at[n],
            recv_sem=recv_sem.at[n],
            device_id=device,
            device_id_type=MESH,
        )
        copy.start()
        started.append(copy)
        return copy

    def exchange(source, target, devices):
        return [send(source.at[s + 1], target.at[s + 1], devices[s]) for s in range(3)]

    def arrive(copies):
        for copy in copies:
            copy.wait_recv()

    def place(ref, tensor):
        for g, part in enumerate(blocks(tensor)):
            ref[g] = part

    def whole(ref):
        return jnp.concatenate([ref[g] for g in range(4)], axis=0)

    root = 1.0 / math.sqrt(32.0)
    channels = w_proj.shape[0]
    coarse = w_cproj.shape[0]

    classes = dot(to_parity[...], surface_in[...])
    surface = jnp.dot(classes, table[...], precision=lax.Precision.HIGHEST)
    base = dot(to_parity[...], fields[...]) + surface
    normed = layer_norm(base, gain_attn[...]).astype(BF16)
    place(norm_send, dot(to_quadrant[...], normed).astype(BF16))
    norm_win[0] = norm_send[0]
    pl.semaphore_wait(barrier, len(greeted))
    moves = exchange(norm_send, norm_win, ahead)

    cot = dot(to_parity[...], cotangent[...])
    cot_bf = blocks(cot.astype(BF16))
    grad_cnext = sum(
        dot_nt(cot_bf[g], w_up[:, g * channels : (g + 1) * channels]) for g in range(4)
    )
    grad_cout = dot_nt(grad_cnext.astype(BF16), w_cproj[...]).astype(BF16)
    key_ids = iota((FINE, FINE), 0)
    query_ids = iota((FINE, FINE), 1)
    edge = jnp.where(i == 0, 1, 0)
    same = (key_ids // (2 * PAD) - query_ids // (2 * PAD)) * edge == 0
    real = key_ids % PAD < 36
    fine_bias = jnp.where(jnp.logical_and(same, real), 0.0, -1e30)
    coarse_bias = jnp.where(real, 0.0, -1e30)
    head_f = iota((FINE, channels), 1) // 32

    arrive(moves)
    rolled = whole(norm_win)
    w_q = w_qkv[:, :channels]
    w_k = w_qkv[:, channels : 2 * channels]
    w_v = w_qkv[:, 2 * channels :]
    q = dot(rolled, w_q).astype(BF16)
    k = dot(rolled, w_k).astype(BF16)
    v = dot(rolled, w_v).astype(BF16)
    zero = jnp.zeros_like(q)
    v_turned = dot_nt(eye[...], v).astype(BF16)
    att_turned = []
    for h in range(HEADS_F):
        scores = dot_nt(jnp.where(head_f == h, k, zero), q) * root + fine_bias
        expon = jnp.exp(scores - jnp.max(scores, axis=0, keepdims=True))
        probs = expon * (1.0 / jnp.sum(expon, axis=0, keepdims=True))
        probs_f[h] = probs
        att_turned.append(dot(v_turned[32 * h : 32 * h + 32], probs.astype(BF16)))
    att = dot_nt(eye[...], jnp.concatenate(att_turned, axis=0).astype(BF16)).astype(BF16)

    place(att_win, att)
    att_back[0] = att_win[0]
    moves = exchange(att_win, att_back, behind)
    arrive(moves)
    restored = dot(from_quadrant[...], whole(att_back)).astype(BF16)

    first = base + dot(restored, w_proj[...])
    mlp_in = layer_norm(first, gain_mlp[...]).astype(BF16)
    pre = dot(mlp_in, w_in[...])
    second = first + dot(gelu_tanh(pre).astype(BF16), w_out[...])

    merged = blocks(second)
    gains = [gain_merge[:, g * channels : (g + 1) * channels] for g in range(4)]
    average = wide_mean(merged)
    centred = [part - average for part in merged]
    inverse = lax.rsqrt(wide_mean([part * part for part in centred]) + epsilon)
    normal = [part * inverse for part in centred]
    coarse_base = sum(
        dot((normal[g] * gains[g]).astype(BF16), w_merge[g * channels : (g + 1) * channels, :])
        for g in range(4)
    )
    coarse_norm = layer_norm(coarse_base, gain_coarse[...]).astype(BF16)
    kv[0] = dot(coarse_norm, w_cqkv[:, coarse:]).astype(BF16)
    moves = [send(kv.at[0], kv.at[s + 1], group[s]) for s in range(3)]
    cq = dot(coarse_norm, w_cqkv[:, :coarse]).astype(BF16)
    block_rows = iota((FINE, 128), 0) // PAD
    own_head = block_rows == iota((FINE, 128), 1) // 32
    own_turned = iota((128, FINE), 0) // 32 == iota((128, FINE), 1) // PAD

    def spread(part):
        tall = jnp.concatenate([part] * 4, axis=0)
        return jnp.where(own_head, tall, jnp.zeros_like(tall))

    spread_q = [spread(cq[:, 128 * g : 128 * g + 128]) for g in range(3)]
    spread_do = [spread(grad_cout[:, 128 * g : 128 * g + 128]) for g in range(3)]
    arrive(moves)

    keys = whole(kv.at[:, :, :coarse])
    values = whole(kv.at[:, :, coarse:])
    score_grads = []
    for g in range(3):
        lanes = slice(128 * g, 128 * g + 128)
        scores = dot_nt(keys[:, lanes], spread_q[g]) * root + coarse_bias
        expon = jnp.exp(scores - jnp.max(scores, axis=0, keepdims=True))
        probs = expon * (1.0 / jnp.sum(expon, axis=0, keepdims=True))
        probs_c[g] = probs.astype(BF16)
        soft_grad = dot_nt(values[:, lanes], spread_do[g])
        kept = jnp.sum(soft_grad * probs, axis=0, keepdims=True)
        score_grad = (probs * (soft_grad - kept)).astype(BF16)
        score_grads.append(score_grad)
        grad_v = dot(probs_c[g], spread_do[g])
        grad_k = dot(score_grad, spread_q[g]) * root
        for s in range(4):
            rows = slice(s * PAD, (s + 1) * PAD)
            gkv_send[s, :, 128 * g : 128 * g + 128] = grad_k[rows].astype(BF16)
            gkv_send[s, :, coarse + 128 * g : coarse + 128 * g + 128] = grad_v[rows].astype(BF16)
    moves = exchange(gkv_send, gkv_recv, group)

    grad_cqs, outs = [], []
    for g in range(3):
        lanes = slice(128 * g, 128 * g + 128)
        small = eye[:128, :128]
        turned = dot(dot_nt(small, keys[:, lanes]).astype(BF16), score_grads[g]) * root
        grad_cqs.append(dot_nt(fold[...], jnp.where(own_turned, turned, 0.0).astype(BF16)))
        turned = dot(dot_nt(small, values[:, lanes]).astype(BF16), probs_c[g])
        outs.append(dot_nt(fold[...], jnp.where(own_turned, turned, 0.0).astype(BF16)))
    coarse_out = jnp.concatenate(outs, axis=1).astype(BF16)
    coarse_next = (coarse_base + dot(coarse_out, w_cproj[...])).astype(BF16)
    upward = jnp.concatenate(
        [dot(coarse_next, w_up[:, g * channels : (g + 1) * channels]) for g in range(4)], axis=0
    )
    pred_out[...] = dot(to_natural[...], (second + upward).astype(BF16)).astype(BF16)
    grad_cq = jnp.concatenate(grad_cqs, axis=1).astype(BF16)
    grad_cnorm = dot_nt(grad_cq, w_cqkv[:, :coarse])

    arrive(moves)
    grad_kv = gkv_send[0].astype(F32)
    for s in range(1, 4):
        grad_kv = grad_kv + gkv_recv[s].astype(F32)
    grad_cnorm = grad_cnorm + dot_nt(grad_kv.astype(BF16), w_cqkv[:, coarse:])
    grad_cbase = grad_cnext + layer_norm_back(coarse_base, gain_coarse[...], grad_cnorm)
    grad_cbase = grad_cbase.astype(BF16)
    scaled = [
        dot_nt(grad_cbase, w_merge[g * channels : (g + 1) * channels, :]) * gains[g]
        for g in range(4)
    ]
    mean_scaled = wide_mean(scaled)
    mean_both = wide_mean([scaled[g] * normal[g] for g in range(4)])
    grad_merged = [
        inverse * (scaled[g] - mean_scaled - normal[g] * mean_both) for g in range(4)
    ]
    grad_second = cot + jnp.concatenate(grad_merged, axis=0)
    grad_active = dot_nt(grad_second.astype(BF16), w_out[...])
    grad_pre = (grad_active * gelu_slope(pre)).astype(BF16)
    grad_mlp_in = dot_nt(grad_pre, w_in[...])
    grad_first = grad_second + layer_norm_back(first, gain_mlp[...], grad_mlp_in)
    grad_first_bf = grad_first.astype(BF16)
    grad_restored = dot_nt(grad_first_bf, w_proj[...]).astype(BF16)
    place(gres_send, dot(to_quadrant[...], grad_restored).astype(BF16))
    gres_win[0] = gres_send[0]
    moves = exchange(gres_send, gres_win, ahead)
    grad_proj = dot(dot_nt(eye[...], restored).astype(BF16), grad_first_bf)
    k_turned = dot_nt(eye[...], k).astype(BF16)
    rolled_turned = dot_nt(eye[...], rolled).astype(BF16)
    arrive(moves)

    do = whole(gres_win)
    grad_v = jnp.zeros((FINE, channels), F32)
    grad_k = jnp.zeros((FINE, channels), F32)
    gq_turned = []
    for h in range(HEADS_F):
        mine = head_f == h
        probs = probs_f[h]
        soft_grad = dot_nt(jnp.where(mine, v, zero), do)
        kept = jnp.sum(soft_grad * probs, axis=0, keepdims=True)
        score_grad = (probs * (soft_grad - kept)).astype(BF16)
        grad_v = grad_v + dot(probs.astype(BF16), jnp.where(mine, do, zero))
        grad_k = grad_k + dot(score_grad, jnp.where(mine, q, zero))
        gq_turned.append(dot(k_turned[32 * h : 32 * h + 32], score_grad) * root)
    grad_q = dot_nt(eye[...], jnp.concatenate(gq_turned, axis=0).astype(BF16)).astype(BF16)
    grad_k = (grad_k * root).astype(BF16)
    grad_v = grad_v.astype(BF16)
    grad_rolled = dot_nt(grad_q, w_q) + dot_nt(grad_k, w_k) + dot_nt(grad_v, w_v)
    place(groll_win, grad_rolled.astype(BF16))
    groll_back[0] = groll_win[0]
    moves = exchange(groll_win, groll_back, behind)

    part_q = dot(rolled_turned, grad_q)
    part_k = dot(rolled_turned, grad_k)
    part_v = dot(rolled_turned, grad_v)
    if reduces:
        for g in range(4):
            rows = slice(g * PAD, (g + 1) * PAD)
            reduce_send[g, :, :channels] = part_q[rows].astype(BF16)
            reduce_send[g, :, channels:] = part_k[rows].astype(BF16)
            reduce_send[4 + g, :, :channels] = part_v[rows].astype(BF16)
            reduce_send[4 + g, :, channels:] = grad_proj[rows].astype(BF16)
        me = i * 4 + j % 4
        to_owner = [
            send(reduce_send.at[lat * 4 + lon % 4], reduce_recv.at[d], (lon, lat))
            for d, (lon, lat) in enumerate(plane)
        ]
    else:
        gqkv_out[:, :channels] = part_q
        gqkv_out[:, channels : 2 * channels] = part_k
        gqkv_out[:, 2 * channels :] = part_v
        gproj_out[...] = grad_proj

    arrive(moves)
    grad_normed = dot(from_quadrant[...], whole(groll_back))
    grad_base = grad_first + layer_norm_back(base, gain_attn[...], grad_normed)
    gin_out[...] = dot(to_natural[...], grad_base.astype(BF16)).astype(BF16)

    if reduces:
        arrive(to_owner)
        total = reduce_send[me].astype(F32)
        for d in range(7):
            total = total + reduce_recv[d].astype(F32)
        line_send[...] = total.astype(BF16)
        moves = [send(line_send, line_recv.at[d], line[d]) for d in range(3)]
        arrive(moves)
        total = (line_send[...].astype(F32) + line_recv[0].astype(F32)) + (
            line_recv[1].astype(F32) + line_recv[2].astype(F32)
        )
        gathered[me] = total.astype(BF16)
        moves = [send(gathered.at[me], gathered.at[me], device) for device in plane]
        arrive(moves)
        for g in range(4):
            rows = slice(g * PAD, (g + 1) * PAD)
            left = gathered[g].astype(F32)
            right = gathered[4 + g].astype(F32)
            gqkv_out[rows, : 2 * channels] = left
            gqkv_out[rows, 2 * channels :] = right[:, :channels]
            gproj_out[rows, :] = right[:, channels:]
    for copy in started:
        copy.wait_send()

def per_device(
    sizes,
    fields,
    cotangent,
    land_sea,
    orography,
    land_vec,
    orog_table,
    gain_attn,
    w_qkv,
    w_proj,
    gain_mlp,
    w_in,
    w_out,
    gain_merge,
    w_merge,
    gain_coarse,
    w_cqkv,
    w_cproj,
    w_up,
):
    reduces = sizes[2]
    channels = fields.shape[-1]
    coarse = w_cproj.shape[0]
    tokens = 2 * WLAT * WLON
    kinds = orog_table.shape[0]
    lanes = jnp.arange(128, dtype=jnp.int32)
    land = jnp.where(lanes == kinds, land_sea.reshape(-1, 1), 0)
    classes = jnp.where(lanes == orography.reshape(-1, 1), 1, land).astype(BF16)
    classes = jnp.concatenate([classes, classes], axis=0)
    table = jnp.concatenate(
        [orog_table, land_vec[None], jnp.zeros((127 - kinds, channels), F32)], axis=0
    )
    operands = [
        fields.reshape(tokens, channels),
        cotangent.reshape(tokens, channels),
        classes,
        table,
        gain_attn[None],
        w_qkv,
        w_proj,
        gain_mlp[None],
        w_in,
        w_out,
        gain_merge[None],
        w_merge,
        gain_coarse[None],
        w_cqkv,
        w_cproj,
        w_up,
        *orderings(),
    ]
    tile = pltpu.VMEM((4, PAD, channels), BF16)
    wide = pltpu.VMEM((4, PAD, 2 * coarse), BF16)
    prediction, grad_input, grad_qkv, grad_proj = pl.pallas_call(
        functools.partial(kernel, sizes),
        out_shape=(
            jax.ShapeDtypeStruct((tokens, channels), BF16),
            jax.ShapeDtypeStruct((tokens, channels), BF16),
            jax.ShapeDtypeStruct((channels, 3 * channels), F32),
            jax.ShapeDtypeStruct((channels, channels), F32),
        ),
        in_specs=[pl.BlockSpec(memory_space=pltpu.VMEM)] * len(operands),
        out_specs=[pl.BlockSpec(memory_space=pltpu.VMEM)] * 4,
        scratch_shapes=[
            tile,
            tile,
            tile,
            tile,
            wide,
            wide,
            wide,
            tile,
            tile,
            tile,
            tile,
            pltpu.VMEM((HEADS_F, FINE, FINE), F32),
            pltpu.VMEM((3, FINE, FINE), BF16),
            pltpu.VMEM((8, PAD, 2 * channels), BF16),
            pltpu.VMEM((7, PAD, 2 * channels), BF16),
            pltpu.VMEM((PAD, 2 * channels), BF16),
            pltpu.VMEM((3, PAD, 2 * channels), BF16),
            pltpu.VMEM((8, PAD, 2 * channels), BF16),
            pltpu.SemaphoreType.DMA((35,)),
            pltpu.SemaphoreType.DMA((35,)),
        ],
        compiler_params=pltpu.CompilerParams(
            collective_id=0, has_side_effects=True, vmem_limit_bytes=48 * 2**20
        ),
    )(*operands)
    if not reduces:
        grad_qkv, grad_proj = lax.psum((grad_qkv, grad_proj), ("lon", "lat"))
    return (
        prediction.reshape(fields.shape),
        grad_input.reshape(fields.shape),
        grad_qkv,
        grad_proj,
    )

def solution(mesh):
    lat_size, lon_size = mesh.shape["lat"], mesh.shape["lon"]
    sizes = (lat_size, lon_size, lat_size == 2 and lon_size == 16)
    split = P(None, "lat", "lon", None)
    placed = (split, split, P("lat", "lon"), P("lat", "lon")) + (P(),) * 14
    return jax.shard_map(
        functools.partial(per_device, sizes),
        mesh=mesh,
        in_specs=placed,
        out_specs=(split, split, P(), P()),
        check_vma=False,
    )
```

time: 228 us -> 69.9 us (0.31)
  waiting for transfers between devices: 146 us -> 0 us
  Pallas kernels: 0 us -> 50 us
  matrix products: 20.2 us -> 0 us
  between operations: 15.1 us -> 0.79 us
  starting transfers between devices: 12.6 us -> 0 us
  local copies, waits for them, and re-layouts: 28.2 us -> 17.5 us
  other arithmetic: 5.21 us -> 0.91 us
    psum x1 -> x0, waiting for transfers between devices: 123 us -> none  [per_device(): grad_qkv, grad_proj = lax.psum((qkv_local, proj_local), ('lon', 'lat'))]
    pallas_call x0 -> x1, Pallas kernels: none -> 50 us  [per_device(): pl.pallas_call(functools.partial(kernel, sizes), out_shape=(jax.ShapeDtyp...]
    ppermute x12 -> x0, waiting for transfers between devices: 22.4 us -> none  [the longest x8 20.4 us: from_behind(): return lax.ppermute(block, axis, route)]
    dot_general x27 -> x0, matrix products: 18.3 us -> none  [the longest x2 3.8 us: attend_back(): jnp.einsum('whqk,wqhd->wkhd', soft_bf, grad_heads, preferred_element_type...]
    ppermute x12 -> x0, starting transfers between devices: 12.5 us -> none  [the longest x8 7.98 us: from_behind(): return lax.ppermute(block, axis, route)]
    reshape x9 -> x4, local copies, waits for them, and re-layouts: 3.74 us -> 0.13 us  [the longest x1 0.04 us: per_device(): fields.reshape(tokens, channels)]
    unnamed x138 -> x37, local copies, waits for them, and re-layouts: 17.1 us -> 14.3 us
    convert_element_type x7 -> x1, other arithmetic: 2.6 us -> 0.08 us  [per_device(): classes = jnp.where(lanes == orography.reshape(-1, 1), 1, land).astype(BF16)]
  transfers between devices with their start and end apart: 13 -> 0, of which waited for: 9 -> 0; matrix products, arithmetic and copies ran while one was open for 4% -> 0% of each run, Pallas kernels for 0% -> 0%
where the time goes in v1:
time: 69.9 us; the launch traced here: 69.2 us
  Pallas kernels  50 us (72%)
  local copies, waits for them, and re-layouts  17.5 us (25%)
  other arithmetic  0.91 us (1%)
  between operations  0.79 us (1%)
    pallas_call x1, Pallas kernels, per_device(): pl.pallas_call(functools.partial(kernel, sizes), out_shape=(jax.ShapeDtyp...  50 us
    unnamed x37, local copies, waits for them, and re-layouts  14.3 us

profile of v1, /device:TPU:0, one launch (start us, length us, event | category | flops | bytes accessed | tf_op | source)
XLA Modules:
  0.0 69.2 jit_solution(3629526358389449190)
XLA Ops:
  0.6 0.0 copy-start
  0.6 0.8 %broadcast_in_dim.43 = s32[72]{0:T(128)S(1)} reshape(s32[6,12]{1,0:T(8,128)} %param.26) | data formatting | bytes 576 | tf_op jit(solution)/shard_map/jit(_where)/broadcast_in_dim | solution.py:457
  1.5 0.8 %eq.22 = s32[72]{0:T(128)S(1)} reshape(s32[6,12]{1,0:T(8,128)} %param.27) | data formatting | bytes 576 | tf_op jit(solution)/shard_map/eq | solution.py:458
  2.3 0.1 pad.2.clone
  2.3 0.7 broadcast_in_dim.51.gain_coarse
  3.0 0.7 broadcast_in_dim.50.gain_merge
  3.7 0.1 select_convert_fusion
  3.8 0.9 %copy.33 = bf16[2,6,12,192]{3,2,1,0:T(8,128)(2,1)S(1)} copy(bf16[2,6,12,192]{3,0,2,1:T(2,128)(2,1)} %param.24) | data formatting | bytes 110592 | tf_op args[0]
  4.8 0.0 copy-start.1
  4.8 1.0 %copy.34 = bf16[2,6,12,192]{3,2,1,0:T(8,128)(2,1)S(1)} copy(bf16[2,6,12,192]{3,0,2,1:T(2,128)(2,1)} %param.25) | data formatting | bytes 110592 | tf_op args[1]
  5.8 0.8 %maximum_maximum_fusion.table = f32[128,192]{1,0:T(8,128)S(1)} fusion(f32[1,192]{1,0:T(1,128)} %bitcast.5, f32[16,192]{1,0:T(8,128)} %param.29, f32[128]{0:T(128)S(1)} %pad.2.clone), kind=kLoop, calls=%fused_computation | loop fusion | flops 49152 | bytes 111872 | tf_op jit(solution)/shard_map/concatenate | solution.py:460
  6.6 0.0 copy-start.6
  6.6 0.0 copy-start.12
  6.6 0.0 copy-start.13
  6.6 0.0 copy-start.14
  6.6 1.2 %copy.35.w_out = bf16[768,192]{1,0:T(8,128)(2,1)S(1)} copy(bf16[768,192]{0,1:T(8,128)(2,1)} %param.35) | data formatting | bytes 589824 | tf_op args[11]
  7.8 0.0 copy-done
  7.8 0.0 copy-done.1
  7.8 0.0 copy-done.6
  7.9 0.0 copy-done.12
  7.9 0.0 copy-done.13
  7.9 0.0 copy-done.14
  7.9 0.0 copy-start.2
  7.9 1.1 %copy-done.2 = bf16[384,768]{1,0:T(8,128)(2,1)S(1)} copy-done((bf16[384,768]{1,0:T(8,128)(2,1)S(1)}, bf16[384,768]{1,0:T(8,128)(2,1)}, u32[]{:S(2)}) %copy-start.2) | copy-done | bytes 589848
  9.0 0.0 copy-start.3
  9.0 1.0 %copy-done.3 = bf16[192,768]{1,0:T(8,128)(2,1)S(1)} copy-done((bf16[192,768]{1,0:T(8,128)(2,1)S(1)}, bf16[192,768]{1,0:T(8,128)(2,1)}, u32[]{:S(2)}) %copy-start.3) | copy-done | bytes 294936
  9.9 0.0 copy-start.4
  9.9 1.0 %copy-done.4 = bf16[384,384]{1,0:T(8,128)(2,1)S(1)} copy-done((bf16[384,384]{1,0:T(8,128)(2,1)S(1)}, bf16[384,384]{1,0:T(8,128)(2,1)}, u32[]{:S(2)}) %copy-start.4) | copy-done | bytes 294936
  10.9 0.0 copy-start.5
  10.9 0.9 %copy-done.5 = bf16[192,576]{1,0:T(8,128)(2,1)S(1)} copy-done((bf16[192,576]{1,0:T(8,128)(2,1)S(1)}, bf16[192,576]{1,0:T(8,128)(2,1)}, u32[]{:S(2)}) %copy-start.5) | copy-done | bytes 221208
  11.8 0.0 copy-start.7
  11.8 0.9 %copy-done.7 = bf16[192,192]{1,0:T(8,128)(2,1)S(1)} copy-done((bf16[192,192]{1,0:T(8,128)(2,1)S(1)}, bf16[192,192]{1,0:T(8,128)(2,1)}, u32[]{:S(2)}) %copy-start.7) | copy-done | bytes 73752
  12.7 0.0 copy-start.8
  12.7 0.9 %copy-done.8 = bf16[192,192]{1,0:T(8,128)(2,1)S(1)} copy-done((bf16[192,192]{1,0:T(8,128)(2,1)S(1)}, bf16[192,192]{1,0:T(8,128)(2,1)}, u32[]{:S(2)}) %copy-start.8) | copy-done | bytes 73752
  13.6 0.0 copy-start.9
  13.6 0.9 %copy-done.9 = bf16[192,192]{1,0:T(8,128)(2,1)S(1)} copy-done((bf16[192,192]{1,0:T(8,128)(2,1)S(1)}, bf16[192,192]{1,0:T(8,128)(2,1)}, u32[]{:S(2)}) %copy-start.9) | copy-done | bytes 73752
  14.5 0.0 copy-start.10
  14.5 0.9 %copy-done.10 = bf16[192,144]{1,0:T(8,128)(2,1)S(1)} copy-done((bf16[192,144]{1,0:T(8,128)(2,1)S(1)}, bf16[192,144]{1,0:T(8,128)(2,1)}, u32[]{:S(2)}) %copy-start.10) | copy-done | bytes 55320
  15.4 0.0 copy-start.11
  15.4 0.9 %copy-done.11 = bf16[144,192]{1,0:T(8,128)(2,1)S(1)} copy-done((bf16[144,192]{1,0:T(8,128)(2,1)S(1)}, bf16[144,192]{1,0:T(8,128)(2,1)}, u32[]{:S(2)}) %copy-start.11) | copy-done | bytes 55320
  16.3 50.0 %shard_map.255 = (bf16[144,192]{1,0:T(8,128)(2,1)S(1)}, bf16[144,192]{1,0:T(8,128)(2,1)S(1)}, f32[192,576]{1,0:T(8,128)S(1)}, f32[192,192]{1,0:T(8,128)S(1)}) custom-call(bf16[144,192]{1,0:T(8,128)(2,1)S(1)} %reshape.24.fields, bf16[144,192]{1,0:T(8,128)(2,1)S(1)} %reshape.25.cotangent, bf16[144,128]{1,0:T(8,128)(2,1)S(1)} %pad_maximum_fusion.surface_in, ...), custom_call_target="tpu_custom_call" | custom-call | tf_op jit(solution)/shard_map/pallas_call | solution.py:484
  66.3 0.7 %copy.36 = bf16[2,6,12,192]{3,0,2,1:T(2,128)(2,1)} copy(bf16[2,6,12,192]{3,2,1,0:T(8,128)(2,1)S(1)} %reshape.26) | data formatting | bytes 110592
  67.1 0.7 %copy.37 = bf16[2,6,12,192]{3,0,2,1:T(2,128)(2,1)} copy(bf16[2,6,12,192]{3,2,1,0:T(8,128)(2,1)S(1)} %reshape.27) | data formatting | bytes 110592
  67.8 0.8 %copy.40 = f32[192,576]{1,0:T(8,128)} copy(f32[192,576]{1,0:T(8,128)S(1)} %get-tuple-element.26) | data formatting | bytes 884736
  68.6 0.7 copy.41
  (7 shorter events, 0.1 us)
Async XLA Ops:
  0.6 7.2 %copy-start = (bf16[384,1152]{1,0:T(8,128)(2,1)S(1)}, bf16[384,1152]{1,0:T(8,128)(2,1)}, u32[]{:S(2)}) copy-start(bf16[384,1152]{1,0:T(8,128)(2,1)} %w_cqkv.1) | copy-start | bytes 2654212
  4.8 3.1 %copy-start.1 = (bf16[768,384]{1,0:T(8,128)(2,1)S(1)}, bf16[768,384]{1,0:T(8,128)(2,1)}, u32[]{:S(2)}) copy-start(bf16[768,384]{1,0:T(8,128)(2,1)} %w_merge.1) | copy-start | bytes 1769476
  6.6 1.3 %copy-start.6 = (bf16[192,192]{1,0:T(8,128)(2,1)S(1)}, bf16[192,192]{1,0:T(8,128)(2,1)}, u32[]{:S(2)}) copy-start(bf16[192,192]{1,0:T(8,128)(2,1)} %w_proj.1) | copy-start | bytes 221188
  6.6 1.3 %copy-start.12 = (bf16[48,192]{1,0:T(8,128)(2,1)S(1)}, bf16[48,192]{1,0:T(8,128)(2,1)}, u32[]{:S(2)}) copy-start(bf16[48,192]{1,0:T(8,128)(2,1)} %constant.25.clone.fold) | copy-start | bytes 55300
  6.6 1.2 %copy-start.13 = (f32[192]{0:T(256)S(1)}, f32[192]{0:T(256)}, u32[]{:S(2)}) copy-start(f32[192]{0:T(256)} %param.30) | copy-start | bytes 2308
  6.6 1.2 %copy-start.14 = (f32[192]{0:T(256)S(1)}, f32[192]{0:T(256)}, u32[]{:S(2)}) copy-start(f32[192]{0:T(256)} %param.33) | copy-start | bytes 2308
  7.9 1.1 %copy-start.2 = (bf16[384,768]{1,0:T(8,128)(2,1)S(1)}, bf16[384,768]{1,0:T(8,128)(2,1)}, u32[]{:S(2)}) copy-start(bf16[384,768]{1,0:T(8,128)(2,1)} %w_up.1) | copy-start | bytes 1769476
  9.0 1.0 %copy-start.3 = (bf16[192,768]{1,0:T(8,128)(2,1)S(1)}, bf16[192,768]{1,0:T(8,128)(2,1)}, u32[]{:S(2)}) copy-start(bf16[192,768]{1,0:T(8,128)(2,1)} %w_in.1) | copy-start | bytes 884740
  9.9 1.0 %copy-start.4 = (bf16[384,384]{1,0:T(8,128)(2,1)S(1)}, bf16[384,384]{1,0:T(8,128)(2,1)}, u32[]{:S(2)}) copy-start(bf16[384,384]{1,0:T(8,128)(2,1)} %w_cproj.1) | copy-start | bytes 884740
  10.9 0.9 %copy-start.5 = (bf16[192,576]{1,0:T(8,128)(2,1)S(1)}, bf16[192,576]{1,0:T(8,128)(2,1)}, u32[]{:S(2)}) copy-start(bf16[192,576]{1,0:T(8,128)(2,1)} %w_qkv.1) | copy-start | bytes 663556
  11.8 0.9 %copy-start.7 = (bf16[192,192]{1,0:T(8,128)(2,1)S(1)}, bf16[192,192]{1,0:T(8,128)(2,1)}, u32[]{:S(2)}) copy-start(bf16[192,192]{1,0:T(8,128)(2,1)} %constant.24.clone.eye) | copy-start | bytes 221188
  12.7 0.9 %copy-start.8 = (bf16[192,192]{1,0:T(8,128)(2,1)S(1)}, bf16[192,192]{1,0:T(8,128)(2,1)}, u32[]{:S(2)}) copy-start(bf16[192,192]{1,0:T(8,128)(2,1)} %constant.23.clone.from_quadrant) | copy-start | bytes 221188
  13.6 0.9 %copy-start.9 = (bf16[192,192]{1,0:T(8,128)(2,1)S(1)}, bf16[192,192]{1,0:T(8,128)(2,1)}, u32[]{:S(2)}) copy-start(bf16[192,192]{1,0:T(8,128)(2,1)} %constant.22.clone.to_quadrant) | copy-start | bytes 221188
  14.5 0.9 %copy-start.10 = (bf16[192,144]{1,0:T(8,128)(2,1)S(1)}, bf16[192,144]{1,0:T(8,128)(2,1)}, u32[]{:S(2)}) copy-start(bf16[192,144]{1,0:T(8,128)(2,1)} %constant.20.clone.to_parity) | copy-start | bytes 165892
  15.4 0.9 %copy-start.11 = (bf16[144,192]{1,0:T(8,128)(2,1)S(1)}, bf16[144,192]{1,0:T(8,128)(2,1)}, u32[]{:S(2)}) copy-start(bf16[144,192]{1,0:T(8,128)(2,1)} %constant.21.clone.to_natural) | copy-start | bytes 165892

commit v2 on v1

v2 whole, which is shorter than its diff:
```python
import functools
import math

import jax
import jax.numpy as jnp
import numpy as np
from jax import lax
from jax.experimental import pallas as pl
from jax.experimental.pallas import tpu as pltpu
from jax.sharding import PartitionSpec as P

HEADS_F = 6
WLAT = 6
WLON = 12
PAD = 48
FINE = 4 * PAD
TOKENS = 2 * WLAT * WLON
MESH = pl.DeviceIdType.MESH
F32 = jnp.float32
BF16 = jnp.bfloat16

epsilon = 1e-05
gelu_coeff = 0.7978845608028654


def layer_norm(values, gain_vec):
    average = jnp.mean(values, axis=-1, keepdims=True)
    centred = values - average
    spread = jnp.mean(centred * centred, axis=-1, keepdims=True)
    return centred * lax.rsqrt(spread + epsilon) * gain_vec


def layer_norm_back(values, gain_vec, upstream):
    average = jnp.mean(values, axis=-1, keepdims=True)
    centred = values - average
    spread = jnp.mean(centred * centred, axis=-1, keepdims=True)
    inverse = lax.rsqrt(spread + epsilon)
    normal = centred * inverse
    scaled = upstream * gain_vec
    return inverse * (
        scaled
        - jnp.mean(scaled, axis=-1, keepdims=True)
        - normal * jnp.mean(scaled * normal, axis=-1, keepdims=True)
    )


def gelu_tanh(values):
    inner = gelu_coeff * (values + 0.044715 * values * values * values)
    return 0.5 * values * (1.0 + jnp.tanh(inner))


def gelu_slope(values):
    inner = gelu_coeff * (values + 0.044715 * values * values * values)
    tangent = jnp.tanh(inner)
    return 0.5 * (1.0 + tangent) + 0.5 * values * (1.0 - tangent * tangent) * gelu_coeff * (
        1.0 + 3.0 * 0.044715 * values * values
    )


def iota(shape, axis):
    return lax.broadcasted_iota(jnp.int32, shape, axis)


def one_hot(rows, cols):
    return jnp.where(rows == cols, 1.0, 0.0).astype(BF16)


def natural_of(parity):
    group, place = parity // PAD, parity % PAD
    row = place // 6 % 3 * 2 + group // 2
    col = place % 6 * 2 + group % 2
    return jnp.where(place < 36, (row * WLON + col) * 2 + place // 18, -1)


def parity_of(quadrant):
    corner, place = quadrant // PAD, quadrant % PAD
    row = place // 6 % 3 + corner // 2 * 3
    col = place % 6 + corner % 2 * 6
    spot = (place // 18 * 3 + row // 2) * 6 + col // 2
    return jnp.where(place < 36, (row % 2 * 2 + col % 2) * PAD + spot, -1)


def dot(a, b):
    return jnp.dot(a, b, preferred_element_type=F32)

def dot_nt(a, b):
    return lax.dot_general(a, b, (((1,), (1,)), ((), ())), preferred_element_type=F32)

def blocks(tensor):
    return [tensor[g * PAD : (g + 1) * PAD] for g in range(4)]

def wide_mean(parts):
    total = parts[0]
    for part in parts[1:]:
        total = total + part
    return jnp.sum(total, axis=-1, keepdims=True) * (1.0 / (4 * total.shape[-1]))

def row_of(ref):
    return ref[...].reshape(1, -1)


def flip(index, bit):
    return index + bit * (1 - 2 * (index // bit % 2))

NAMES = (
    "orography",
    "land_sea",
    "both",
    "table",
    "land_vec",
    "gain_attn",
    "w_qkv",
    "w_up",
    "w_cproj",
    "w_proj",
    "gain_mlp",
    "w_in",
    "w_out",
    "gain_merge",
    "w_merge",
    "gain_coarse",
    "w_cqkv",
)


VMEM_BYTES = 61 * 2**20


def kernel(sizes, *refs):
    count = len(NAMES)
    sources = refs[:count]
    pred_out, gin_out, gqkv_out, gproj_out = refs[count : count + 4]
    local = refs[count + 4 : 2 * count + 4]
    (
        norm_send,
        norm_win,
        att_win,
        att_back,
        heads_send,
        heads_recv,
        back_send,
        back_recv,
        joined,
        gres_send,
        gres_win,
        groll_win,
        groll_back,
        probs_f,
        reduce_send,
        reduce_recv,
        line_send,
        line_recv,
        gathered,
        send_sem,
        recv_sem,
        load_sem,
    ) = refs[2 * count + 4 :]
    loads = {
        name: pltpu.make_async_copy(sources[n], local[n], load_sem.at[n])
        for n, name in enumerate(NAMES)
    }
    for name in NAMES:
        loads[name].start()

    def need(*names):
        refs_of = []
        for name in names:
            loads[name].wait()
            refs_of.append(local[NAMES.index(name)])
        return refs_of

    lat_size, lon_size, reduces = sizes
    i = lax.axis_index("lat")
    j = lax.axis_index("lon")

    def at(lat, lon):
        return (lax.rem(lon + lon_size, lon_size), lax.rem(lat + lat_size, lat_size))

    ahead = [at(i, j + 1), at(i + 1, j), at(i + 1, j + 1)]
    behind = [at(i, j - 1), at(i - 1, j), at(i - 1, j - 1)]
    group = [(flip(j, 1), i), (j, flip(i, 1)), (flip(j, 1), flip(i, 1))]
    greeted = ahead + behind + group
    plane, line = [], []
    if reduces:
        for d in range(1, 8):
            lat = flip(i, 1) if d & 4 else i
            lon = flip(j, 2) if d & 2 else j
            lon = flip(lon, 1) if d & 1 else lon
            plane.append((lon, lat))
        for d in range(1, 4):
            lon = flip(j, 8) if d & 2 else j
            lon = flip(lon, 4) if d & 1 else lon
            line.append((lon, i))
        greeted = greeted + plane + line
    barrier = pltpu.get_barrier_semaphore()
    for device in greeted:
        pl.semaphore_signal(barrier, inc=1, device_id=device, device_id_type=MESH)

    started = []

    def send(source, target, device):
        n = len(started)
        copy = pltpu.make_async_remote_copy(
            src_ref=source,
            dst_ref=target,
            send_sem=send_sem.at[n],
            recv_sem=recv_sem.at[n],
            device_id=device,
            device_id_type=MESH,
        )
        copy.start()
        started.append(copy)
        return copy

    def exchange(source, target, devices):
        return [send(source.at[s + 1], target.at[s + 1], devices[s]) for s in range(3)]

    def arrive(copies):
        for copy in copies:
            copy.wait_recv()

    def place(ref, tensor):
        for g, part in enumerate(blocks(tensor)):
            ref[g] = part

    def whole(ref):
        return jnp.concatenate([ref[g] for g in range(4)], axis=0)

    root = 1.0 / math.sqrt(32.0)

    def give(out, tensor):
        out[...] = dot(to_natural, tensor.astype(BF16)).astype(BF16)

    upright, along = iota((FINE, 1), 0), iota((1, FINE), 1)
    to_parity = one_hot(natural_of(upright), along[:, :TOKENS])
    to_natural = one_hot(upright[:TOKENS], natural_of(along))
    to_quadrant = one_hot(parity_of(upright), along)
    from_quadrant = one_hot(upright, parity_of(along))
    eye = one_hot(upright, along)
    orography, land_sea, both = need("orography", "land_sea", "both")
    pick_row = iota((TOKENS, WLAT), 0) // (2 * WLON) == iota((TOKENS, WLAT), 1)
    pick_row = jnp.where(pick_row, 1.0, 0.0).astype(BF16)
    pick_col = iota((TOKENS, WLON), 0) // 2 % WLON == iota((TOKENS, WLON), 1)

    def per_token(ref):
        rows = dot(pick_row, ref[...].astype(F32).astype(BF16))
        return jnp.sum(jnp.where(pick_col, rows, 0.0), axis=1, keepdims=True)

    table, land_vec, gain_attn = need("table", "land_vec", "gain_attn")
    kinds = table.shape[0]
    lanes = iota((TOKENS, 128), 1).astype(F32)
    land = jnp.where(lanes == kinds, per_token(land_sea), 0.0)
    classes = jnp.where(lanes == per_token(orography), 1.0, land).astype(BF16)
    classes = dot(to_parity, classes)
    surface = jnp.dot(classes[:, :kinds], table[...], precision=lax.Precision.HIGHEST)
    surface = classes[:, kinds : kinds + 1] * row_of(land_vec) + surface
    base = dot(to_parity, both[0]) + surface
    normed = layer_norm(base, row_of(gain_attn)).astype(BF16)
    place(norm_send, dot(to_quadrant, normed).astype(BF16))
    norm_win[0] = norm_send[0]
    pl.semaphore_wait(barrier, len(greeted))
    moves = exchange(norm_send, norm_win, ahead)

    w_up, w_cproj = need("w_up", "w_cproj")
    channels = w_up.shape[1] // 4
    coarse = w_cproj.shape[0]
    cot = dot(to_parity, both[1])
    cot_bf = blocks(cot.astype(BF16))
    grad_cnext = sum(
        dot_nt(cot_bf[g], w_up[:, g * channels : (g + 1) * channels]) for g in range(4)
    )
    grad_cout = dot_nt(grad_cnext.astype(BF16), w_cproj[...]).astype(BF16)
    share = coarse // 4

    def hand_out(column, tensor):
        for r in range(4):
            heads_send[r, :, column * share : (column + 1) * share] = tensor[
                :, r * share : (r + 1) * share
            ]

    hand_out(3, grad_cout)
    key_ids = iota((FINE, FINE), 0)
    query_ids = iota((FINE, FINE), 1)
    edge = jnp.where(i == 0, 1, 0)
    same = (key_ids // (2 * PAD) - query_ids // (2 * PAD)) * edge == 0
    real = key_ids % PAD < 36
    fine_bias = jnp.where(jnp.logical_and(same, real), 0.0, -1e30)
    coarse_bias = jnp.where(real, 0.0, -1e30)
    head_f = iota((FINE, channels), 1) // 32

    arrive(moves)
    rolled = whole(norm_win)
    (w_qkv,) = need("w_qkv")
    w_q = w_qkv[:, :channels]
    w_k = w_qkv[:, channels : 2 * channels]
    w_v = w_qkv[:, 2 * channels :]
    q = dot(rolled, w_q).astype(BF16)
    k = dot(rolled, w_k).astype(BF16)
    v = dot(rolled, w_v).astype(BF16)
    zero = jnp.zeros_like(q)
    v_turned = dot_nt(eye, v).astype(BF16)
    att_turned = []
    for h in range(HEADS_F):
        scores = dot_nt(jnp.where(head_f == h, k, zero), q) * root + fine_bias
        expon = jnp.exp(scores - jnp.max(scores, axis=0, keepdims=True))
        probs = expon * (1.0 / jnp.sum(expon, axis=0, keepdims=True))
        probs_f[h] = probs
        att_turned.append(dot(v_turned[32 * h : 32 * h + 32], probs.astype(BF16)))
    att = dot_nt(eye, jnp.concatenate(att_turned, axis=0).astype(BF16)).astype(BF16)

    place(att_win, att)
    att_back[0] = att_win[0]
    moves = exchange(att_win, att_back, behind)
    w_proj, gain_mlp, w_in, w_out, gain_merge, w_merge, gain_coarse, w_cqkv = need("w_proj", "gain_mlp", "w_in", "w_out", "gain_merge", "w_merge", "gain_coarse", "w_cqkv")
    arrive(moves)
    restored = dot(from_quadrant, whole(att_back)).astype(BF16)

    first = base + dot(restored, w_proj[...])
    mlp_in = layer_norm(first, row_of(gain_mlp)).astype(BF16)
    pre = dot(mlp_in, w_in[...])
    second = first + dot_nt(gelu_tanh(pre).astype(BF16), w_out[...])

    merged = blocks(second)
    gain_row = row_of(gain_merge)
    gains = [gain_row[:, g * channels : (g + 1) * channels] for g in range(4)]
    average = wide_mean(merged)
    centred = [part - average for part in merged]
    inverse = lax.rsqrt(wide_mean([part * part for part in centred]) + epsilon)
    normal = [part * inverse for part in centred]
    coarse_base = sum(
        dot((normal[g] * gains[g]).astype(BF16), w_merge[g * channels : (g + 1) * channels, :])
        for g in range(4)
    )
    coarse_norm = layer_norm(coarse_base, row_of(gain_coarse)).astype(BF16)
    coarse_qkv = dot(coarse_norm, w_cqkv[...]).astype(BF16)
    for column in range(3):
        hand_out(column, coarse_qkv[:, column * coarse : (column + 1) * coarse])
    rank = i % 2 * 2 + j % 2
    moves = [
        send(heads_send.at[lat % 2 * 2 + lon % 2], heads_recv.at[s + 1], (lon, lat))
        for s, (lon, lat) in enumerate(group)
    ]
    heads_recv[0] = heads_send[rank]
    arrive(moves)

    gathered_in = whole(heads_recv)
    cq, ck, cv, cdo = (gathered_in[:, n * share : (n + 1) * share] for n in range(4))
    head_c = iota((FINE, share), 1) // 32
    none = jnp.zeros_like(cq)
    cv_turned = dot_nt(eye[:share, :share], cv).astype(BF16)
    ck_turned = dot_nt(eye[:share, :share], ck).astype(BF16)
    grad_cv = jnp.zeros((FINE, share), F32)
    grad_ck = jnp.zeros((FINE, share), F32)
    turned = []
    for h in range(share // 32):
        mine = head_c == h
        scores = dot_nt(jnp.where(mine, ck, none), cq) * root + coarse_bias
        expon = jnp.exp(scores - jnp.max(scores, axis=0, keepdims=True))
        probs = expon * (1.0 / jnp.sum(expon, axis=0, keepdims=True))
        soft = probs.astype(BF16)
        soft_grad = dot_nt(jnp.where(mine, cv, none), cdo)
        kept = jnp.sum(soft_grad * probs, axis=0, keepdims=True)
        score_grad = (probs * (soft_grad - kept)).astype(BF16)
        grad_cv = grad_cv + dot(soft, jnp.where(mine, cdo, none))
        grad_ck = grad_ck + dot(score_grad, jnp.where(mine, cq, none))
        rows = slice(32 * h, 32 * h + 32)
        turned.append((dot(ck_turned[rows], score_grad) * root, dot(cv_turned[rows], soft)))
    grad_cq, coarse_out = (
        dot_nt(eye, jnp.concatenate(part, axis=0).astype(BF16)) for part in zip(*turned)
    )
    results = (grad_cq, grad_ck * root, grad_cv, coarse_out)
    for n, part in enumerate(results):
        for s in range(4):
            rows = slice(s * PAD, (s + 1) * PAD)
            back_send[s, :, n * share : (n + 1) * share] = part[rows].astype(BF16)
    moves = [
        send(back_send.at[s + 1], back_recv.at[rank], device) for s, device in enumerate(group)
    ]
    back_recv[rank] = back_send[0]
    arrive(moves)

    for n in range(4):
        for r in range(4):
            start = n * coarse + r * share
            joined[:, start : start + share] = back_recv[r, :, n * share : (n + 1) * share]
    grad_cnorm = dot_nt(joined[:, : 3 * coarse], w_cqkv[...])
    grad_cbase = grad_cnext + layer_norm_back(coarse_base, row_of(gain_coarse), grad_cnorm)
    grad_cbase = grad_cbase.astype(BF16)
    scaled = [
        dot_nt(grad_cbase, w_merge[g * channels : (g + 1) * channels, :]) * gains[g]
        for g in range(4)
    ]
    mean_scaled = wide_mean(scaled)
    mean_both = wide_mean([scaled[g] * normal[g] for g in range(4)])
    grad_merged = [
        inverse * (scaled[g] - mean_scaled - normal[g] * mean_both) for g in range(4)
    ]
    grad_second = cot + jnp.concatenate(grad_merged, axis=0)
    grad_active = dot(grad_second.astype(BF16), w_out[...])
    grad_pre = (grad_active * gelu_slope(pre)).astype(BF16)
    grad_mlp_in = dot_nt(grad_pre, w_in[...])
    grad_first = grad_second + layer_norm_back(first, row_of(gain_mlp), grad_mlp_in)
    grad_first_bf = grad_first.astype(BF16)
    grad_restored = dot_nt(grad_first_bf, w_proj[...]).astype(BF16)
    place(gres_send, dot(to_quadrant, grad_restored).astype(BF16))
    gres_win[0] = gres_send[0]
    moves = exchange(gres_send, gres_win, ahead)
    grad_proj = dot(dot_nt(eye, restored).astype(BF16), grad_first_bf)
    coarse_next = (coarse_base + dot(joined[:, 3 * coarse :], w_cproj[...])).astype(BF16)
    upward = jnp.concatenate(
        [dot(coarse_next, w_up[:, g * channels : (g + 1) * channels]) for g in range(4)], axis=0
    )
    give(pred_out, second + upward)
    k_turned = dot_nt(eye, k).astype(BF16)
    rolled_turned = dot_nt(eye, rolled).astype(BF16)
    arrive(moves)

    do = whole(gres_win)
    grad_v = jnp.zeros((FINE, channels), F32)
    grad_k = jnp.zeros((FINE, channels), F32)
    gq_turned = []
    for h in range(HEADS_F):
        mine = head_f == h
        probs = probs_f[h]
        soft_grad = dot_nt(jnp.where(mine, v, zero), do)
        kept = jnp.sum(soft_grad * probs, axis=0, keepdims=True)
        score_grad = (probs * (soft_grad - kept)).astype(BF16)
        grad_v = grad_v + dot(probs.astype(BF16), jnp.where(mine, do, zero))
        grad_k = grad_k + dot(score_grad, jnp.where(mine, q, zero))
        gq_turned.append(dot(k_turned[32 * h : 32 * h + 32], score_grad) * root)
    grad_q = dot_nt(eye, jnp.concatenate(gq_turned, axis=0).astype(BF16)).astype(BF16)
    grad_k = (grad_k * root).astype(BF16)
    grad_v = grad_v.astype(BF16)
    grad_rolled = dot_nt(grad_q, w_q) + dot_nt(grad_k, w_k) + dot_nt(grad_v, w_v)
    place(groll_win, grad_rolled.astype(BF16))
    groll_back[0] = groll_win[0]
    moves = exchange(groll_win, groll_back, behind)

    part_q = dot(rolled_turned, grad_q)
    part_k = dot(rolled_turned, grad_k)
    part_v = dot(rolled_turned, grad_v)
    if reduces:
        for g in range(4):
            rows = slice(g * PAD, (g + 1) * PAD)
            reduce_send[g, :, :channels] = part_q[rows].astype(BF16)
            reduce_send[g, :, channels:] = part_k[rows].astype(BF16)
            reduce_send[4 + g, :, :channels] = part_v[rows].astype(BF16)
            reduce_send[4 + g, :, channels:] = grad_proj[rows].astype(BF16)
        me = i * 4 + j % 4
        to_owner = [
            send(reduce_send.at[lat * 4 + lon % 4], reduce_recv.at[d], (lon, lat))
            for d, (lon, lat) in enumerate(plane)
        ]
    else:
        gqkv_out[:, :channels] = part_q
        gqkv_out[:, channels : 2 * channels] = part_k
        gqkv_out[:, 2 * channels :] = part_v
        gproj_out[...] = grad_proj

    arrive(moves)
    grad_normed = dot(from_quadrant, whole(groll_back))
    grad_base = grad_first + layer_norm_back(base, row_of(gain_attn), grad_normed)
    give(gin_out, grad_base)

    if reduces:
        arrive(to_owner)
        total = reduce_send[me].astype(F32)
        for d in range(7):
            total = total + reduce_recv[d].astype(F32)
        line_send[...] = total.astype(BF16)
        moves = [send(line_send, line_recv.at[d], line[d]) for d in range(3)]
        arrive(moves)
        total = (line_send[...].astype(F32) + line_recv[0].astype(F32)) + (
            line_recv[1].astype(F32) + line_recv[2].astype(F32)
        )
        gathered[me] = total.astype(BF16)
        moves = [send(gathered.at[me], gathered.at[me], device) for device in plane]
        arrive(moves)
        for g in range(4):
            rows = slice(g * PAD, (g + 1) * PAD)
            left = gathered[g].astype(F32)
            right = gathered[4 + g].astype(F32)
            gqkv_out[rows, : 2 * channels] = left
            gqkv_out[rows, 2 * channels :] = right[:, :channels]
            gproj_out[rows, :] = right[:, channels:]
    for copy in started:
        copy.wait_send()

def per_device(
    sizes,
    fields,
    cotangent,
    land_sea,
    orography,
    land_vec,
    orog_table,
    gain_attn,
    w_qkv,
    w_proj,
    gain_mlp,
    w_in,
    w_out,
    gain_merge,
    w_merge,
    gain_coarse,
    w_cqkv,
    w_cproj,
    w_up,
):
    reduces = sizes[2]
    channels = fields.shape[-1]
    coarse = w_cproj.shape[0]
    def flat(tensor):
        return tensor.transpose(1, 2, 0, 3).reshape(TOKENS, channels)

    both = jnp.stack([flat(fields), flat(cotangent)])
    known = dict(
        orography=orography,
        land_sea=land_sea,
        both=both,
        table=orog_table,
        land_vec=land_vec,
        gain_attn=gain_attn,
        w_qkv=w_qkv,
        w_up=w_up,
        w_cproj=w_cproj,
        w_proj=w_proj,
        gain_mlp=gain_mlp,
        w_in=w_in,
        w_out=w_out.T,
        gain_merge=gain_merge,
        w_merge=w_merge,
        gain_coarse=gain_coarse,
        w_cqkv=w_cqkv,
    )
    operands = [known[name] for name in NAMES]
    tile = pltpu.VMEM((4, PAD, channels), BF16)
    wide = pltpu.VMEM((4, PAD, coarse), BF16)
    prediction, grad_input, grad_qkv, grad_proj = pl.pallas_call(
        functools.partial(kernel, sizes),
        out_shape=(
            jax.ShapeDtypeStruct((TOKENS, channels), BF16),
            jax.ShapeDtypeStruct((TOKENS, channels), BF16),
            jax.ShapeDtypeStruct((channels, 3 * channels), F32),
            jax.ShapeDtypeStruct((channels, channels), F32),
        ),
        in_specs=[pl.BlockSpec(memory_space=pltpu.HBM)] * len(operands),
        out_specs=[pl.BlockSpec(memory_space=pltpu.VMEM)] * 4,
        scratch_shapes=[pltpu.VMEM(x.shape, x.dtype) for x in operands]
        + [
            tile,
            tile,
            tile,
            tile,
            wide,
            wide,
            wide,
            wide,
            pltpu.VMEM((PAD, 4 * coarse), BF16),
            tile,
            tile,
            tile,
            tile,
            pltpu.VMEM((HEADS_F, FINE, FINE), F32),
            pltpu.VMEM((8, PAD, 2 * channels), BF16),
            pltpu.VMEM((7, PAD, 2 * channels), BF16),
            pltpu.VMEM((PAD, 2 * channels), BF16),
            pltpu.VMEM((3, PAD, 2 * channels), BF16),
            pltpu.VMEM((8, PAD, 2 * channels), BF16),
            pltpu.SemaphoreType.DMA((35,)),
            pltpu.SemaphoreType.DMA((35,)),
            pltpu.SemaphoreType.DMA((len(operands),)),
        ],
        compiler_params=pltpu.CompilerParams(
            collective_id=0, has_side_effects=True, vmem_limit_bytes=VMEM_BYTES
        ),
    )(*operands)
    if not reduces:
        grad_qkv, grad_proj = lax.psum((grad_qkv, grad_proj), ("lon", "lat"))

    def unflat(tensor):
        return tensor.reshape(WLAT, WLON, 2, channels).transpose(2, 0, 1, 3)

    return (
        unflat(prediction),
        unflat(grad_input),
        grad_qkv,
        grad_proj,
    )

def solution(mesh):
    lat_size, lon_size = mesh.shape["lat"], mesh.shape["lon"]
    sizes = (lat_size, lon_size, lat_size == 2 and lon_size == 16)
    split = P(None, "lat", "lon", None)
    placed = (split, split, P("lat", "lon"), P("lat", "lon")) + (P(),) * 14
    return jax.shard_map(
        functools.partial(per_device, sizes),
        mesh=mesh,
        in_specs=placed,
        out_specs=(split, split, P(), P()),
        check_vma=False,
    )
```

time: 69.9 us -> 57 us (0.82)
  local copies, waits for them, and re-layouts: 17.5 us -> 5.89 us
    unnamed x37 -> x8, local copies, waits for them, and re-layouts: 14.3 us -> 2.57 us
    broadcast_in_dim x4 -> x0, local copies, waits for them, and re-layouts: 2.22 us -> none  [the longest x1 0.84 us: per_device(): land = jnp.where(lanes == kinds, land_sea.reshape(-1, 1), 0)]
    reshape x4 -> x2, local copies, waits for them, and re-layouts: 0.13 us -> 2.27 us  [unflat(): return tensor.reshape(WLAT, WLON, 2, channels).transpose(2, 0, 1, 3)]
    another operation x0 -> x2, local copies, waits for them, and re-layouts: none -> 1.06 us  [per_device(): both = jnp.stack([flat(fields), flat(cotangent)])]
    concatenate x2 -> x0, other arithmetic: 0.82 us -> none  [the longest x1 0.81 us: per_device(): jnp.concatenate([orog_table, land_vec[None], jnp.zeros((127 - kinds, chan...]
    eq x1 -> x0, local copies, waits for them, and re-layouts: 0.76 us -> none  [per_device(): classes = jnp.where(lanes == orography.reshape(-1, 1), 1, land).astype(BF16)]
where the time goes in v2:
time: 57 us; the launch traced here: 56.8 us
  Pallas kernels  49.5 us (87%)
  local copies, waits for them, and re-layouts  5.89 us (10%)
  other arithmetic  0.69 us (1%)
  between operations  0.67 us (1%)
    pallas_call x1, Pallas kernels, per_device(): pl.pallas_call(functools.partial(kernel, sizes), out_shape=(jax.ShapeDtyp...  49.5 us
    unnamed x8, local copies, waits for them, and re-layouts  2.57 us
    reshape x2, local copies, waits for them, and re-layouts, unflat(): return tensor.reshape(WLAT, WLON, 2, channels).transpose(2, 0, 1, 3)  2.27 us

profile of v2, /device:TPU:0, one launch (start us, length us, event | category | flops | bytes accessed | tf_op | source)
XLA Modules:
  0.0 56.8 jit_solution(800465623286239172)
XLA Ops:
  0.6 0.0 copy-start.1
  0.6 1.0 %stack_reshape.6 = bf16[1,144,192]{2,1,0:T(8,128)(2,1)S(1)} reshape(bf16[6,12,2,192]{3,2,1,0:T(2,128)(2,1)} %bitcast.6) | data formatting | bytes 110592 | tf_op jit(solution)/shard_map/stack;reshape | solution.py:516
  1.6 0.0 copy-done.1
  1.6 0.1 stack_reshape.7
  1.7 0.7 %pad_maximum_fusion.refs_2_ = bf16[2,144,192]{2,1,0:T(8,128)(2,1)} fusion(bf16[1,144,192]{2,1,0:T(8,128)(2,1)S(1)} %stack_reshape.7, bf16[1,144,192]{2,1,0:T(8,128)(2,1)S(1)} %stack_reshape.6), kind=kLoop, calls=%fused_computation | loop fusion | flops 55296 | bytes 221184 | tf_op jit(solution)/shard_map/stack | solution.py:516
  2.4 49.5 %shard_map.201 = (bf16[144,192]{1,0:T(8,128)(2,1)}, bf16[144,192]{1,0:T(8,128)(2,1)}, f32[192,576]{1,0:T(8,128)}, f32[192,192]{1,0:T(8,128)}) custom-call(s32[6,12]{1,0:T(8,128)} %refs_0_.1, s32[6,12]{1,0:T(8,128)} %refs_1_.1, bf16[2,144,192]{2,1,0:T(8,128)(2,1)} %pad_maximum_fusion.refs_2_, f32[16,192]{1,0:T(8,128)} %refs_3_.1, f32[192]{0:T(256)} %refs_4_.1, ...), custom_call_target="tpu_custom_call" | custom-call | tf_op jit(solution)/shard_map/pallas_call | solution.py:539
  51.9 0.0 copy-start.2
  51.9 1.6 %reshape.14 = bf16[6,12,2,192]{3,2,1,0:T(2,128)(2,1)} reshape(bf16[144,192]{1,0:T(8,128)(2,1)} %get-tuple-element.8) | data formatting | bytes 110592 | tf_op jit(solution)/shard_map/reshape | solution.py:582
  53.5 0.0 copy-done.2
  53.5 0.7 %reshape.15 = bf16[6,12,2,192]{3,2,1,0:T(2,128)(2,1)} reshape(bf16[144,192]{1,0:T(8,128)(2,1)S(1)} %copy-done.2) | data formatting | bytes 110592 | tf_op jit(solution)/shard_map/reshape | solution.py:582
  54.2 0.0 copy-start
  54.2 1.9 %copy.24 = f32[192,576]{1,0:T(8,128)} copy(f32[192,576]{1,0:T(8,128)} %get-tuple-element.18) | data formatting | bytes 884736
  56.1 0.0 copy-done
  56.1 0.7 %copy.25 = f32[192,192]{1,0:T(8,128)} copy(f32[192,192]{1,0:T(8,128)S(1)} %copy-done) | data formatting | bytes 294912
Async XLA Ops:
  0.6 1.0 %copy-start.1 = (bf16[2,6,12,192]{3,0,2,1:T(2,128)(2,1)S(1)}, bf16[2,6,12,192]{3,0,2,1:T(2,128)(2,1)}, u32[]{:S(2)}) copy-start(bf16[2,6,12,192]{3,0,2,1:T(2,128)(2,1)} %param.19) | copy-start | bytes 165892
  51.9 1.6 %copy-start.2 = (bf16[144,192]{1,0:T(8,128)(2,1)S(1)}, bf16[144,192]{1,0:T(8,128)(2,1)}, u32[]{:S(2)}) copy-start(bf16[144,192]{1,0:T(8,128)(2,1)} %get-tuple-element.9) | copy-start | bytes 165892
  54.2 1.9 %copy-start = (f32[192,192]{1,0:T(8,128)S(1)}, f32[192,192]{1,0:T(8,128)}, u32[]{:S(2)}) copy-start(f32[192,192]{1,0:T(8,128)} %get-tuple-element.19) | copy-start | bytes 442372

commit v3 on v2

--- a/solution.py
+++ b/solution.py
@@ -478,8 +478,8 @@
         arrive(moves)
         for g in range(4):
             rows = slice(g * PAD, (g + 1) * PAD)
-            left = gathered[g].astype(F32)
-            right = gathered[4 + g].astype(F32)
+            left = gathered[g]
+            right = gathered[4 + g]
             gqkv_out[rows, : 2 * channels] = left
             gqkv_out[rows, 2 * channels :] = right[:, :channels]
             gproj_out[rows, :] = right[:, channels:]
@@ -534,6 +534,7 @@
         w_cqkv=w_cqkv,
     )
     operands = [known[name] for name in NAMES]
+    sum_type = BF16 if reduces else F32
     tile = pltpu.VMEM((4, PAD, channels), BF16)
     wide = pltpu.VMEM((4, PAD, coarse), BF16)
     prediction, grad_input, grad_qkv, grad_proj = pl.pallas_call(
@@ -541,8 +542,8 @@
         out_shape=(
             jax.ShapeDtypeStruct((TOKENS, channels), BF16),
             jax.ShapeDtypeStruct((TOKENS, channels), BF16),
-            jax.ShapeDtypeStruct((channels, 3 * channels), F32),
-            jax.ShapeDtypeStruct((channels, channels), F32),
+            jax.ShapeDtypeStruct((channels, 3 * channels), sum_type),
+            jax.ShapeDtypeStruct((channels, channels), sum_type),
         ),
         in_specs=[pl.BlockSpec(memory_space=pltpu.HBM)] * len(operands),
         out_specs=[pl.BlockSpec(memory_space=pltpu.VMEM)] * 4,
@@ -584,8 +585,8 @@
     return (
         unflat(prediction),
         unflat(grad_input),
-        grad_qkv,
-        grad_proj,
+        grad_qkv.astype(F32),
+        grad_proj.astype(F32),
     )
 
 def solution(mesh):

time: 57 us -> 56.4 us (0.989)
  local copies, waits for them, and re-layouts: 5.89 us -> 2.82 us
  other arithmetic: 0.69 us -> 3.17 us
    convert_element_type x0 -> x2, other arithmetic: none -> 2.48 us  [the longest x1 1.79 us: per_device(): grad_qkv.astype(F32)]
    unnamed x8, local copies, waits for them, and re-layouts: 2.57 us -> 0.41 us
    reshape x2, local copies, waits for them, and re-layouts: 2.27 us -> 1.35 us  [unflat(): return tensor.reshape(WLAT, WLON, 2, channels).transpose(2, 0, 1, 3)]
where the time goes in v3:
time: 56.4 us; the launch traced here: 56.1 us
  Pallas kernels  49.4 us (88%)
  other arithmetic  3.17 us (6%)
  local copies, waits for them, and re-layouts  2.82 us (5%)
  between operations  0.67 us (1%)
    pallas_call x1, Pallas kernels, per_device(): pl.pallas_call(functools.partial(kernel, sizes), out_shape=(jax.ShapeDtyp...  49.4 us
    convert_element_type x1, other arithmetic, per_device(): grad_qkv.astype(F32)  1.79 us
    reshape x2, local copies, waits for them, and re-layouts, unflat(): return tensor.reshape(WLAT, WLON, 2, channels).transpose(2, 0, 1, 3)  1.35 us

profile of v3, /device:TPU:0, one launch (start us, length us, event | category | flops | bytes accessed | tf_op | source)
XLA Modules:
  0.0 56.1 jit_solution(8445604690517211291)
XLA Ops:
  0.6 0.0 copy-start.1
  0.6 1.0 %stack_reshape.6 = bf16[1,144,192]{2,1,0:T(8,128)(2,1)S(1)} reshape(bf16[6,12,2,192]{3,2,1,0:T(2,128)(2,1)} %bitcast.6) | data formatting | bytes 110592 | tf_op jit(solution)/shard_map/stack;reshape | solution.py:516
  1.6 0.0 copy-done.1
  1.6 0.1 stack_reshape.7
  1.7 0.7 %pad_maximum_fusion.refs_2_ = bf16[2,144,192]{2,1,0:T(8,128)(2,1)} fusion(bf16[1,144,192]{2,1,0:T(8,128)(2,1)S(1)} %stack_reshape.7, bf16[1,144,192]{2,1,0:T(8,128)(2,1)S(1)} %stack_reshape.6), kind=kLoop, calls=%fused_computation | loop fusion | flops 55296 | bytes 221184 | tf_op jit(solution)/shard_map/stack | solution.py:516
  2.4 49.4 %shard_map.201 = (bf16[144,192]{1,0:T(8,128)(2,1)}, bf16[144,192]{1,0:T(8,128)(2,1)}, bf16[192,576]{1,0:T(8,128)(2,1)}, bf16[192,192]{1,0:T(8,128)(2,1)}) custom-call(s32[6,12]{1,0:T(8,128)} %refs_0_.1, s32[6,12]{1,0:T(8,128)} %refs_1_.1, bf16[2,144,192]{2,1,0:T(8,128)(2,1)} %pad_maximum_fusion.refs_2_, f32[16,192]{1,0:T(8,128)} %refs_3_.1, f32[192]{0:T(256)} %refs_4_.1, ...), custom_call_target="tpu_custom_call" | custom-call | tf_op jit(solution)/shard_map/pallas_call | solution.py:540
  51.9 0.0 copy-start
  51.9 1.8 %convert_element_type.6 = f32[192,576]{1,0:T(8,128)} convert(bf16[192,576]{1,0:T(8,128)(2,1)} %get-tuple-element.10) | non-fusion elementwise | flops 110592 | bytes 663552 | tf_op jit(solution)/shard_map/convert_element_type | solution.py:588
  53.7 0.0 copy-done
  53.7 0.0 copy-start.3
  53.7 0.7 %convert_element_type.7 = f32[192,192]{1,0:T(8,128)} convert(bf16[192,192]{1,0:T(8,128)(2,1)S(1)} %copy-done) | non-fusion elementwise | flops 36864 | bytes 221184 | tf_op jit(solution)/shard_map/convert_element_type | solution.py:589
  54.3 0.2 copy-done.3
  54.5 0.0 copy-start.2
  54.5 0.7 %reshape.14 = bf16[6,12,2,192]{3,2,1,0:T(2,128)(2,1)} reshape(bf16[144,192]{1,0:T(8,128)(2,1)S(1)} %copy-done.3) | data formatting | bytes 110592 | tf_op jit(solution)/shard_map/reshape | solution.py:583
  55.2 0.2 copy-done.2
  55.4 0.7 %reshape.15 = bf16[6,12,2,192]{3,2,1,0:T(2,128)(2,1)} reshape(bf16[144,192]{1,0:T(8,128)(2,1)S(1)} %copy-done.2) | data formatting | bytes 110592 | tf_op jit(solution)/shard_map/reshape | solution.py:583
Async XLA Ops:
  0.6 1.0 %copy-start.1 = (bf16[2,6,12,192]{3,0,2,1:T(2,128)(2,1)S(1)}, bf16[2,6,12,192]{3,0,2,1:T(2,128)(2,1)}, u32[]{:S(2)}) copy-start(bf16[2,6,12,192]{3,0,2,1:T(2,128)(2,1)} %param.19) | copy-start | bytes 165892
  51.9 1.8 %copy-start = (bf16[192,192]{1,0:T(8,128)(2,1)S(1)}, bf16[192,192]{1,0:T(8,128)(2,1)}, u32[]{:S(2)}) copy-start(bf16[192,192]{1,0:T(8,128)(2,1)} %get-tuple-element.11) | copy-start | bytes 221188
  53.7 0.9 %copy-start.3 = (bf16[144,192]{1,0:T(8,128)(2,1)S(1)}, bf16[144,192]{1,0:T(8,128)(2,1)}, u32[]{:S(2)}) copy-start(bf16[144,192]{1,0:T(8,128)(2,1)} %get-tuple-element.8) | copy-start | bytes 165892
  54.5 0.9 %copy-start.2 = (bf16[144,192]{1,0:T(8,128)(2,1)S(1)}, bf16[144,192]{1,0:T(8,128)(2,1)}, u32[]{:S(2)}) copy-start(bf16[144,192]{1,0:T(8,128)(2,1)} %get-tuple-element.9) | copy-start | bytes 165892
